TPU v7x, 256 devices: a whole 4x4x8 slice. The times are simulated.
256 devices in a mesh: seq: 16 (over z, core), tensor: 16 (over y, x).
Axes of the slice: x: 4, y: 4, z: 8, core: 2. Of those that a mesh axis runs over, the one named last changes fastest.
Arguments:
- hidden_states: bfloat16 [24576, 8192], P('seq', 'tensor'), may hold values from -600 to 600, as said below
- gate_values: bfloat16 [24576, 8192], P('seq', 'tensor'), may hold values from -6 to 6
- norm_weight: float32 [8192], P('tensor'), may hold values from 0.1 to 1.9
- out_weight: bfloat16 [4096, 8192], P(None, 'tensor'), may hold values from -0.09375 to 0.09375
- out_grad: bfloat16 [24576, 4096], P('seq', 'tensor'), may hold values from -6 to 6
Outputs:
- grad_hidden: bfloat16 [24576, 8192], P('seq', 'tensor')
- grad_gate: bfloat16 [24576, 8192], P('seq', 'tensor')
- grad_out_weight: float32 [4096, 8192], P('seq', 'tensor')
- grad_norm_weight: float32 [8192], P('tensor')
Inputs may be any that keep to these rules, and one draw needn't show every extreme that they name: `hidden_states`: finite values of the state-space scan's output.
All inputs are finite; a program needn't handle non-finite values.
Results may differ from a plain program's by a relative error of at most 0.0031.
Values may be sent and summed in bfloat16 or wider, within the bound.
No kernel may reach another device: no remote copies, remote signals or barrier semaphores. Data moves between devices by JAX's collectives and lax.ppermute only.
A program may use at most 128 MiB of HBM per device.

v0:
```python
import jax
import jax.numpy as jnp
from jax import lax
from jax.experimental import pallas as pl
from jax.experimental.pallas import tpu as pltpu
from jax.sharding import PartitionSpec as P

DI = 8192
BF = jnp.bfloat16
F32 = jnp.float32
AXES = ("seq", "tensor")
SY = SX = 4
SZ = 8
FEAT = 128


def pairs(move):
    table = []
    for z in range(SZ):
        for c in range(2):
            for y in range(SY):
                for x in range(SX):
                    z2, c2, y2, x2 = move(z, c, y, x)
                    target = ((z2 % SZ) * 2 + c2) * 16 + (y2 % SY) * 4 + x2 % SX
                    table.append(((z * 2 + c) * 16 + y * 4 + x, target))
    return table


def first(d):
    return pairs(lambda z, c, y, x: (z, c, y + (d if c else 0), x + (0 if c else d)))


def second(d):
    return pairs(lambda z, c, y, x: (z, c, y + (0 if c else d), x + (d if c else 0)))


def along_z(d):
    return pairs(lambda z, c, y, x: (z + d, c, y, x))


SWAP = pairs(lambda z, c, y, x: (z, 1 - c, y, x))
PARTNER = pairs(lambda z, c, y, x: (z + (1 if (z + c) % 2 == 0 else -1), c, y, x))


def send(value, table):
    return lax.ppermute(value, AXES, table)


def block_ids(core, y0, x0):
    ids = []
    for j in (0, -1, 1, 2):
        for i in (0, -1, 1, 2):
            a = (y0 + j) % 4 * 4 + (x0 + i) % 4
            b = (y0 + i) % 4 * 4 + (x0 + j) % 4
            ids.append(jnp.where(core == 0, a, b))
    return ids


def block_body(groups, operands, has_acc, last, *refs):
    refs = list(refs)
    take = lambda n: [refs.pop(0) for _ in range(n)]
    inner = any(g[3] for g in groups)
    outer = any(g[4] for g in groups)
    (ids,) = take(1)
    stacks = take(operands)
    w = take(1)[0] if inner else None
    normed = take(1)[0] if outer else None
    acc_in = take(1)[0] if has_acc else None
    if last:
        weight, normalized = take(2)
    gn = take(1)[0] if inner else None
    mine, other = take(2) if outer else (None, None)
    stat, gain_ref = take(2) if last else (None, None)
    xs, sx = take(2)
    if inner:
        ws, acc, sw, sg = take(4)
    if outer:
        nv, go, sn, so = take(4)
    if has_acc:
        (sa,) = take(1)
    if last:
        pv, sp = take(2)
    tok = xs.shape[1]
    tile = 512
    tiles = tok // tile

    def feed(g):
        members, base, chunk, with_w, _ = groups[g]
        out = []
        for k in range(4):
            n = 4 * g + k
            ref, index = members[k]
            out.append(
                pltpu.make_async_copy(stacks[ref].at[index], xs.at[g, :, pl.ds(k * FEAT, FEAT)], sx.at[n])
            )
            if with_w:
                row = pl.multiple_of(ids[base + k] * (2 * FEAT) + chunk * FEAT, FEAT)
                out.append(
                    pltpu.make_async_copy(w.at[pl.ds(row, FEAT), :], ws.at[g, pl.ds(k * FEAT, FEAT), :], sw.at[n])
                )
        for copy in out:
            copy.start()
        return out

    waiting = {}
    if outer:
        cn = pltpu.make_async_copy(normed, nv, sn)
        cn.start()
        normed_waited = False
    for g in range(min(2, len(groups))):
        waiting[g] = feed(g)
    if has_acc:
        ca = pltpu.make_async_copy(acc_in, acc, sa)
        ca.start()
    if last:
        cp = pltpu.make_async_copy(normalized, pv, sp)
        cp.start()
    done = []
    slot = 0
    for g, (_, base, chunk, with_w, with_n) in enumerate(groups):
        for copy in waiting[g]:
            copy.wait()
        if g + 2 < len(groups):
            waiting[g + 2] = feed(g + 2)
        if with_n:
            if not normed_waited:
                cn.wait()
                normed_waited = True
            go[slot] = lax.dot_general(
                xs[g], nv[...], (((0,), (0,)), ((), ())), preferred_element_type=F32
            )
            for k in range(4):
                place = ids[16 + base + k]
                piece = go.at[slot, pl.ds(k * FEAT, FEAT), :]
                sem = so.at[4 * slot + k]
                row = pl.multiple_of(place % SZ * FEAT, FEAT)

                @pl.when(place < SZ)
                def _():
                    pltpu.make_async_copy(piece, mine.at[pl.ds(row, FEAT), :], sem).start()

                @pl.when(place >= SZ)
                def _():
                    pltpu.make_async_copy(piece, other.at[pl.ds(row, FEAT), :], sem).start()

                done.append(pltpu.make_async_copy(piece, mine.at[pl.ds(0, FEAT), :], sem))
            slot += 1
        if with_w:
            if g == 0 and has_acc:
                ca.wait()
            for t in range(tiles):
                rows = pl.ds(t * tile, tile)
                part = jnp.dot(xs[g, rows, :], ws[g], preferred_element_type=F32)
                if g == 0 and not has_acc:
                    acc[rows, :] = part
                else:
                    acc[rows, :] += part
                if g == len(groups) - 1:
                    out = pltpu.make_async_copy(acc.at[rows, :], gn.at[rows, :], sg.at[t])
                    out.start()
                    done.append(out)
    if last:
        cp.wait()
        gain = jnp.zeros((1, acc.shape[1]), F32)
        for t in range(tok // 128):
            rows = pl.ds(t * 128, 128)
            q = acc[rows, :] * pv[rows, :]
            gain += jnp.sum(q, axis=0, keepdims=True)
            q = q * weight[...]
            folded = q[:, 0:128] + q[:, 128:256] + q[:, 256:384] + q[:, 384:512]
            stat[:, pl.ds(t * 128, 128)] = jnp.sum(folded.T, axis=0, keepdims=True)
        gain_ref[...] = jnp.broadcast_to(gain, gain_ref.shape)
    for copy in done:
        copy.wait()


def block_kernel(name, ids, stacks, groups, w=None, normed=None, acc=None, ends=None):
    tok, ch = 1536, 512
    inner, outer = w is not None, normed is not None
    count = len(groups)
    outers = sum(g[4] for g in groups)
    has_acc, last = acc is not None, ends is not None
    anyspace = pl.BlockSpec(memory_space=pl.ANY)
    whole = pl.BlockSpec(memory_space=pltpu.VMEM)
    in_specs = [pl.BlockSpec(memory_space=pltpu.SMEM)] + [anyspace] * len(stacks)
    args = [ids, *stacks]
    dma = lambda n: pltpu.SemaphoreType.DMA((n,))
    scratch = [pltpu.VMEM((count, tok, 4 * FEAT), BF), dma(4 * count)]
    out_shape = []
    if inner:
        args.append(w)
        in_specs.append(anyspace)
        scratch += [
            pltpu.VMEM((count, 4 * FEAT, ch), BF), pltpu.VMEM((tok, ch), F32), dma(4 * count), dma(tok // 512),
        ]
        out_shape.append(jax.ShapeDtypeStruct((tok, ch), F32))
    if outer:
        args.append(normed)
        in_specs.append(anyspace)
        scratch += [
            pltpu.VMEM((tok, ch), BF), pltpu.VMEM((outers, 4 * FEAT, ch), F32),
            pltpu.SemaphoreType.DMA(()), dma(4 * outers),
        ]
        out_shape += [jax.ShapeDtypeStruct((SZ * FEAT, ch), F32)] * 2
    out_specs = [anyspace] * len(out_shape)
    if has_acc:
        in_specs.append(anyspace)
        args.append(acc)
        scratch.append(pltpu.SemaphoreType.DMA(()))
    if last:
        args += list(ends)
        in_specs += [whole, anyspace]
        out_shape += [jax.ShapeDtypeStruct((1, tok), F32), jax.ShapeDtypeStruct((8, ch), F32)]
        out_specs += [whole, whole]
        scratch += [pltpu.VMEM((tok, ch), F32), pltpu.SemaphoreType.DMA(())]
    work = 8_000_000_000 * sum(g[3] + g[4] for g in groups)
    return pl.pallas_call(
        lambda *refs: block_body(groups, len(stacks), has_acc, last, *refs),
        out_shape=tuple(out_shape),
        in_specs=in_specs,
        out_specs=tuple(out_specs),
        scratch_shapes=scratch,
        compiler_params=pltpu.CompilerParams(vmem_limit_bytes=48 * 1024 * 1024),
        cost_estimate=pl.CostEstimate(flops=work, bytes_accessed=24_000_000 * count, transcendentals=0),
        name=name,
    )(*args)


def mix_body(mine1, came1, got1, mine2, came2, got2, own, *outs):
    for c, (mine, came, got) in enumerate(((mine1, came1, got1), (mine2, came2, got2))):
        for m, out in ((0, own), (2, outs[0]), (1, outs[1]), (3, outs[2])):
            rows = slice(m * FEAT, m * FEAT + FEAT)
            value = mine[rows, :] + came[rows, :] + got[rows, :].astype(F32)
            out[c * FEAT : (c + 1) * FEAT, :] = value.astype(out.dtype)


def mix(mine1, came1, got1, mine2, came2, got2):
    ch = mine1.shape[1]
    part = pl.BlockSpec((4 * FEAT, ch), lambda i: (0, 0))
    whole = pl.BlockSpec((2 * FEAT, ch), lambda i: (0, 0))
    return pl.pallas_call(
        mix_body,
        grid=(1,),
        out_shape=(jax.ShapeDtypeStruct((2 * FEAT, ch), F32),) + (jax.ShapeDtypeStruct((2 * FEAT, ch), BF),) * 3,
        in_specs=[part] * 6,
        out_specs=(whole,) * 4,
        cost_estimate=pl.CostEstimate(flops=4_000_000, bytes_accessed=8_000_000, transcendentals=0),
        name="mix",
    )(mine1, came1, got1, mine2, came2, got2)


def parts_of(value, axis):
    spread = jnp.broadcast_to(value.reshape(1, -1), (16, value.size))
    return lax.all_to_all(spread, axis, 0, 0, tiled=True)


def total(value, axis):
    return jnp.sum(parts_of(value, axis), axis=0)


def last_body(hidden, gate, grad, normalized, weight, inverse, products, grad_hidden, grad_gate):
    for t in range(hidden.shape[0] // 128):
        part = slice(t * 128, t * 128 + 128)
        row = jnp.sum(products[:, part], axis=0, keepdims=True) / DI
        mean = jnp.broadcast_to(row, (128, 128)).T
        scale = jnp.broadcast_to(inverse[:, part], (128, 128)).T
        for k in range(hidden.shape[1] // 128):
            lanes = slice(k * 128, k * 128 + 128)
            g = gate[part, lanes].astype(F32)
            sigmoid = 0.5 + 0.5 * jnp.tanh(0.5 * g)
            d = scale * (grad[part, lanes] * weight[:, lanes] - normalized[part, lanes] * mean)
            grad_hidden[part, lanes] = (d * (g * sigmoid)).astype(BF)
            slope = sigmoid * (1.0 + g * (1.0 - sigmoid))
            grad_gate[part, lanes] = (d * hidden[part, lanes].astype(F32) * slope).astype(BF)


def last(hidden, gate, grad, normalized, weight, inverse, products):
    tok, ch = hidden.shape
    tile = 512
    wide = pl.BlockSpec((tile, ch), lambda i: (i, 0))
    return pl.pallas_call(
        last_body,
        grid=(tok // tile,),
        out_shape=(jax.ShapeDtypeStruct((tok, ch), BF),) * 2,
        in_specs=[
            wide, wide, wide, wide,
            pl.BlockSpec((1, ch), lambda i: (0, 0)),
            pl.BlockSpec((1, tile), lambda i: (0, i)),
            pl.BlockSpec((16, tile), lambda i: (0, i)),
        ],
        out_specs=(wide, wide),
        cost_estimate=pl.CostEstimate(flops=1_000, bytes_accessed=1_000, transcendentals=0),
        name="last",
    )(hidden, gate, grad, normalized, weight, inverse, products)


def local(hidden_states, gate_values, norm_weight, out_weight, out_grad):
    seq = lax.axis_index("seq")
    place = lax.axis_index("tensor")
    core, z0 = seq % 2, seq // 2
    z1 = (z0 + jnp.where((z0 + core) % 2 == 0, 1, -1)) % SZ
    near = lambda value: [value] + [send(value, first(d)) for d in (1, -1, 2)]
    names = block_ids(core, place // 4, place % 4)
    slots = []
    for b in names:
        z = b // 2
        far = (z - z0) % 2
        side = b % 2
        partner = (z0 + jnp.where((z0 + side) % 2 == 0, 1, -1)) % SZ
        slot = far * 4 + (z - jnp.where(far == 0, z0, partner)) % SZ // 2
        slots.append(jnp.where(side == core, 0, SZ) + slot)
    ids = jnp.stack(names + slots).astype(jnp.int32)

    def gather(value):
        stack = jnp.stack([value] + [send(value, first(d)) for d in (1, -1, 2)])
        right, left = send(stack, second(1)), send(stack, second(-1))
        return stack, right, left, send(right[:2], second(1)), send(left[2:], second(-1))

    set1 = gather(out_grad[:, :FEAT])
    set2 = gather(out_grad[:, FEAT:])

    gate_wide = gate_values.astype(F32)
    sigmoid_gate = jax.nn.sigmoid(gate_wide)
    gate_silu = gate_wide * sigmoid_gate
    hidden_wide = hidden_states.astype(F32)
    gated = hidden_wide * gate_silu
    squares = total(jnp.sum(gated * gated, axis=-1), "tensor")
    inverse_rms = 1.0 / jnp.sqrt(squares / DI + 1e-05)
    normalized = gated * inverse_rms[:, None]
    normed = (normalized * norm_weight).astype(BF)

    def grouped(operand, chunk, with_w, with_n):
        n = operand
        parts = [[(n + j, k) for k in range(4)] for j in range(3)] + [[(n + 3, 0), (n + 3, 1), (n + 4, 0), (n + 4, 1)]]
        return [(parts[k], 4 * k, chunk, with_w, with_n) for k in range(4)]

    half = 4 * FEAT
    mine1, other1 = block_kernel("outer1", ids, set1, grouped(0, 0, 0, 1), None, normed)
    came1 = send(other1, SWAP)
    mine2, other2 = block_kernel("outer2", ids, set2, grouped(0, 1, 0, 1), None, normed)
    came2 = send(other2, SWAP)
    mate1 = (mine1[half:] + came1[half:]).astype(BF)
    mate2 = (mine2[half:] + came2[half:]).astype(BF)
    mate1, mate2, ids1 = lax.optimization_barrier((mate1, mate2, ids))
    got1, got2 = send(mate1, PARTNER), send(mate2, PARTNER)
    grad_normed, stat, gain = block_kernel(
        "inner", ids1, set1 + set2, grouped(0, 0, 1, 0) + grouped(5, 1, 1, 0), out_weight, None, None,
        (norm_weight[None], normalized),
    )
    got1, got2, stat = lax.optimization_barrier((got1, got2, stat))
    own, *outs = mix(mine1, came1, got1, mine2, came2, got2)
    rows = own
    for block, d in zip((outs[1], outs[2], outs[0]), (2, -2, 4)):
        rows = rows + send(block, along_z(d)).astype(F32)
    products = parts_of(stat, "tensor")
    grad_hidden, grad_gate = last(
        hidden_states, gate_values, grad_normed, normalized, norm_weight[None], inverse_rms[None], products
    )
    gain, _ = lax.optimization_barrier((gain[0], products))
    grad_norm_weight = total(gain, "seq")
    return grad_hidden, grad_gate, rows, grad_norm_weight


def solution(mesh):
    return jax.shard_map(
        local,
        mesh=mesh,
        in_specs=(
            P("seq", "tensor"),
            P("seq", "tensor"),
            P("tensor"),
            P(None, "tensor"),
            P("seq", "tensor"),
        ),
        out_specs=(P("seq", "tensor"), P("seq", "tensor"), P("seq", "tensor"), P("tensor")),
        check_vma=False,
    )
```

profile of v0, /device:TPU:1, one launch (start us, length us, event | category | flops | bytes accessed | tf_op | source)
XLA Modules:
  0.0 157.5 jit_solution(13051226790463353845)
XLA Ops:
  0.6 1.3 slice_bitcast_fusion
  2.0 3.6 %collective-permute-start.9 = (bf16[1536,128]{1,0:T(8,128)(2,1)S(1)}, bf16[1536,128]{1,0:T(8,128)(2,1)S(1)}, u32[]{:S(2)}, u32[]{:S(2)}) collective-permute-start(bf16[1536,128]{1,0:T(8,128)(2,1)S(1)} %get-tuple-element.48), channel_id=1, source_target_pairs={{0,3},{1,0},{2,1},{3,2},{4,7},{5,4},{6,5},{7,6},{8,11},{9,8},{10,9... | collective-permute-start | bytes 1179656 | tf_op jit(solution)/shard_map/ppermute | solution.py:46
  5.6 1.6 %collective-permute-start.10 = (bf16[1536,128]{1,0:T(8,128)(2,1)S(1)}, bf16[1536,128]{1,0:T(8,128)(2,1)S(1)}, u32[]{:S(2)}, u32[]{:S(2)}) collective-permute-start(bf16[1536,128]{1,0:T(8,128)(2,1)S(1)} %get-tuple-element.48), channel_id=1, source_target_pairs={{0,2},{1,3},{2,0},{3,1},{4,6},{5,7},{6,4},{7,5},{8,10},{9,11},{10,... | collective-permute-start | bytes 1179656 | tf_op jit(solution)/shard_map/ppermute | solution.py:46
  8.9 5.7 %collective-permute-done.9 = bf16[1536,128]{1,0:T(8,128)(2,1)S(1)} collective-permute-done((bf16[1536,128]{1,0:T(8,128)(2,1)S(1)}, bf16[1536,128]{1,0:T(8,128)(2,1)S(1)}, u32[]{:S(2)}, u32[]{:S(2)}) %collective-permute-start.9) | collective-permute-done | bytes 393248 | tf_op jit(solution)/shard_map/ppermute | solution.py:46
  14.5 3.4 %collective-permute-done.8 = bf16[1536,128]{1,0:T(8,128)(2,1)S(1)} collective-permute-done((bf16[1536,128]{1,0:T(8,128)(2,1)S(1)}, bf16[1536,128]{1,0:T(8,128)(2,1)S(1)}, u32[]{:S(2)}, u32[]{:S(2)}) %collective-permute-start.8) | collective-permute-done | bytes 393248 | tf_op jit(solution)/shard_map/ppermute | solution.py:46
  18.2 2.6 %collective-permute-start.12 = (bf16[4,1536,128]{2,1,0:T(8,128)(2,1)S(1)}, bf16[4,1536,128]{2,1,0:T(8,128)(2,1)}, u32[]{:S(2)}, u32[]{:S(2)}) collective-permute-start(bf16[4,1536,128]{2,1,0:T(8,128)(2,1)S(1)} %pad_maximum_fusion.1.refs_1_.refs_6_), channel_id=1, source_target_pairs={{0,12},{1,13},{2,14},{3,15},{4,0},{5,1},{6,2},{7,3},{8,4},{9,5},{1... | collective-permute-start | bytes 4718600 | tf_op jit(solution)/shard_map/ppermute | solution.py:46
  20.7 5.6 %collective-permute-done = bf16[1536,128]{1,0:T(8,128)(2,1)S(1)} collective-permute-done((bf16[1536,128]{1,0:T(8,128)(2,1)S(1)}, bf16[1536,128]{1,0:T(8,128)(2,1)S(1)}, u32[]{:S(2)}, u32[]{:S(2)}) %collective-permute-start) | collective-permute-done | bytes 393248 | tf_op jit(solution)/shard_map/ppermute | solution.py:46
  26.6 3.5 %collective-permute-start.4 = (bf16[4,1536,128]{2,1,0:T(8,128)(2,1)S(1)}, bf16[4,1536,128]{2,1,0:T(8,128)(2,1)}, u32[]{:S(2)}, u32[]{:S(2)}) collective-permute-start(bf16[4,1536,128]{2,1,0:T(8,128)(2,1)S(1)} %pad_maximum_fusion.refs_1_), channel_id=1, source_target_pairs={{0,12},{1,13},{2,14},{3,15},{4,0},{5,1},{6,2},{7,3},{8,4},{9,5},{1... | collective-permute-start | bytes 4718600 | tf_op jit(solution)/shard_map/ppermute | solution.py:46
  30.1 1.1 multiply_reduce_fusion
  31.9 6.0 %all-to-all-start = ((f32[16,1,1536]{2,1,0:T(1,128)}), f32[16,1,1536]{2,1,0:T(1,128)S(1)}, u32[]{:S(2)}, u32[]{:S(2)}) async-start(f32[16,1,1536]{2,1,0:T(1,128)} %broadcast_in_dim.8), calls=%async_computation | async-start | bytes 196608 | tf_op jit(solution)/shard_map/all_to_all | solution.py:254
  40.5 24.0 %all-to-all-done = f32[16,1,1536]{2,1,0:T(1,128)S(1)} async-done(((f32[16,1,1536]{2,1,0:T(1,128)}), f32[16,1,1536]{2,1,0:T(1,128)S(1)}, u32[]{:S(2)}, u32[]{:S(2)}) %all-to-all-start) | async-done | bytes 98336 | tf_op jit(solution)/shard_map/all_to_all | solution.py:254
  64.6 1.3 slice.48
  66.2 1.2 slice.47
  67.4 1.5 collective-permute-start.13
  69.0 3.3 %multiply_convert_fusion = (bf16[1536,512]{1,0:T(8,128)(2,1)}, f32[1536,512]{1,0:T(8,128)}) fusion(f32[512]{0:T(512)S(1)} %copy-done.1, f32[1536]{0:T(1024)S(1)} %add_rsqrt_fusion, bf16[1536,512]{1,0:T(8,128)(2,1)S(1)} %copy-done.5, bf16[1536,512]{1,0:T(8,128)(2,1)S(1)} %copy-done.3), kind=kLoop, calls=%fused_computation.6 | loop fusion | flops 7864320 | bytes 7872512 | tf_op jit(solution)/shard_map/convert_element_type | solution.py:330
  72.2 1.2 slice.45
  73.4 1.3 collective-permute-start.6
  74.7 1.2 slice.44
  76.2 1.1 collective-permute-done.14.refs_5_.refs_10_
  77.3 2.5 %collective-permute-done.13.refs_4_.refs_9_ = bf16[2,1536,128]{2,1,0:T(8,128)(2,1)S(1)} collective-permute-done((bf16[2,1536,128]{2,1,0:T(8,128)(2,1)S(1)}, bf16[2,1536,128]{2,1,0:T(8,128)(2,1)S(1)}, u32[]{:S(2)}, u32[]{:S(2)}) %collective-permute-start.13) | collective-permute-done | bytes 786464 | tf_op jit(solution)/shard_map/ppermute | solution.py:46
  79.8 7.6 %outer2.1 = (f32[1024,512]{1,0:T(8,128)}, f32[1024,512]{1,0:T(8,128)}) custom-call(s32[32]{0:T(128)S(1)} %stack.161.refs_0_, bf16[4,1536,128]{2,1,0:T(8,128)(2,1)S(1)} %pad_maximum_fusion.1.refs_1_.refs_6_, bf16[4,1536,128]{2,1,0:T(8,128)(2,1)} %collective-permute-done.11.refs_2_.refs_7_, bf16[4,1536,128]{2,1,0:T(8,128)(2,1)} %collective-permute-done.12.refs_3_.refs_8_, ...), custom_call_target="tpu_custom_call" | custom-call | flops 32000000000 | bytes 96000000 | tf_op jit(solution)/shard_map/outer2/pallas_call | solution.py:217
  88.1 7.6 %outer1.1 = (f32[1024,512]{1,0:T(8,128)}, f32[1024,512]{1,0:T(8,128)}) custom-call(s32[32]{0:T(128)S(1)} %stack.161.refs_0_, bf16[4,1536,128]{2,1,0:T(8,128)(2,1)S(1)} %pad_maximum_fusion.refs_1_, bf16[4,1536,128]{2,1,0:T(8,128)(2,1)} %collective-permute-done.3.refs_2_, bf16[4,1536,128]{2,1,0:T(8,128)(2,1)} %collective-permute-done.4.refs_3_, ...), custom_call_target="tpu_custom_call" | custom-call | flops 32000000000 | bytes 96000000 | tf_op jit(solution)/shard_map/outer1/pallas_call | solution.py:217
  96.0 4.1 %collective-permute-done.7.came1 = f32[1024,512]{1,0:T(8,128)S(1)} collective-permute-done((f32[1024,512]{1,0:T(8,128)}, f32[1024,512]{1,0:T(8,128)S(1)}, u32[]{:S(2)}, u32[]{:S(2)}) %collective-permute-start.7) | collective-permute-done | bytes 2097184 | tf_op jit(solution)/shard_map/ppermute | solution.py:46
  100.4 5.8 %collective-permute-start.16 = (bf16[512,512]{1,0:T(8,128)(2,1)S(1)}, bf16[512,512]{1,0:T(8,128)(2,1)S(1)}, u32[]{:S(2)}, u32[]{:S(2)}) collective-permute-start(bf16[512,512]{1,0:T(8,128)(2,1)S(1)} %fusion.5), channel_id=1, source_target_pairs={{0,32},{1,33},{2,34},{3,35},{4,36},{5,37},{6,38},{7,39},{8,40},{9,... | collective-permute-start | bytes 1572872 | tf_op jit(solution)/shard_map/ppermute | solution.py:46
  106.3 11.8 %inner.1 = (f32[1536,512]{1,0:T(8,128)}, f32[1,1536]{1,0:T(1,128)S(1)}, f32[8,512]{1,0:T(8,128)S(1)}) custom-call(s32[32]{0:T(128)S(1)} %stack.161.refs_0_, bf16[4,1536,128]{2,1,0:T(8,128)(2,1)S(1)} %pad_maximum_fusion.refs_1_, bf16[4,1536,128]{2,1,0:T(8,128)(2,1)} %collective-permute-done.3.refs_2_, bf16[4,1536,128]{2,1,0:T(8,128)(2,1)} %collective-permute-done.4.refs_3_, ...), custom_call_target="tpu_custom_call" | custom-call | flops 64000000000 | bytes 192000000 | tf_op jit(solution)/shard_map/inner/pallas_call | solution.py:217
  119.2 3.7 %mix.1 = (f32[256,512]{1,0:T(8,128)}, bf16[256,512]{1,0:T(8,128)(2,1)}, bf16[256,512]{1,0:T(8,128)(2,1)}, bf16[256,512]{1,0:T(8,128)(2,1)}) custom-call(f32[1024,512]{1,0:T(8,128)} %get-tuple-element.24.mine1, f32[1024,512]{1,0:T(8,128)} %copy-done.9, bf16[512,512]{1,0:T(8,128)(2,1)} %copy-done.11, f32[1024,512]{1,0:T(8,128)} %get-tuple-element.26.mine2, ...), custom_call_target="tpu_custom_call" | custom-call | flops 4000000 | bytes 8000000 | tf_op jit(solution)/shard_map/mix/pallas_call | solution.py:241
  122.8 3.6 %collective-permute-start.19 = (bf16[256,512]{1,0:T(8,128)(2,1)}, bf16[256,512]{1,0:T(8,128)(2,1)S(1)}, u32[]{:S(2)}, u32[]{:S(2)}) collective-permute-start(bf16[256,512]{1,0:T(8,128)(2,1)} %get-tuple-element.40), channel_id=1, source_target_pairs={{0,192},{1,193},{2,194},{3,195},{4,196},{5,197},{6,198},{7,199},{8... | collective-permute-start | bytes 786440 | tf_op jit(solution)/shard_map/ppermute | solution.py:46
  126.4 4.1 %collective-permute-start.20 = (bf16[256,512]{1,0:T(8,128)(2,1)}, bf16[256,512]{1,0:T(8,128)(2,1)S(1)}, u32[]{:S(2)}, u32[]{:S(2)}) collective-permute-start(bf16[256,512]{1,0:T(8,128)(2,1)} %get-tuple-element.41), channel_id=1, source_target_pairs={{0,128},{1,129},{2,130},{3,131},{4,132},{5,133},{6,134},{7,135},{8... | collective-permute-start | bytes 786440 | tf_op jit(solution)/shard_map/ppermute | solution.py:46
  131.2 3.5 %all-to-all-start.1 = ((f32[16,1,1536]{2,1,0:T(1,128)}), f32[16,1,1536]{2,1,0:T(1,128)S(1)}, u32[]{:S(2)}, u32[]{:S(2)}) async-start(f32[16,1,1536]{2,1,0:T(1,128)} %broadcast_in_dim.10), calls=%async_computation.1 | async-start | bytes 196608 | tf_op jit(solution)/shard_map/all_to_all | solution.py:254
  134.8 6.8 %all-to-all-done.1 = f32[16,1,1536]{2,1,0:T(1,128)S(1)} async-done(((f32[16,1,1536]{2,1,0:T(1,128)}), f32[16,1,1536]{2,1,0:T(1,128)S(1)}, u32[]{:S(2)}, u32[]{:S(2)}) %all-to-all-start.1) | async-done | bytes 98336 | tf_op jit(solution)/shard_map/all_to_all | solution.py:254
  142.8 5.3 %all-to-all-start.2 = ((f32[16,1,512]{2,1,0:T(1,128)}), f32[16,1,512]{2,1,0:T(1,128)S(1)}, u32[]{:S(2)}, u32[]{:S(2)}) async-start(f32[16,1,512]{2,1,0:T(1,128)} %broadcast_in_dim.11), calls=%async_computation.2 | async-start | bytes 65536 | tf_op jit(solution)/shard_map/all_to_all | solution.py:254
  148.7 7.2 %last.1 = (bf16[1536,512]{1,0:T(8,128)(2,1)}, bf16[1536,512]{1,0:T(8,128)(2,1)}) custom-call(bf16[1536,512]{1,0:T(8,128)(2,1)} %hidden.1, bf16[1536,512]{1,0:T(8,128)(2,1)} %gate.1, f32[1536,512]{1,0:T(8,128)} %get-tuple-element.29.grad, f32[1536,512]{1,0:T(8,128)} %get-tuple-element.45.refs_13_.normalized, f32[1,512]{1,0:T(1,128)} %bitcast.47, ...), custom_call_target="tpu_custom_call" | custom-call | flops 1000 | bytes 1000 | tf_op jit(solution)/shard_map/last/pallas_call | solution.py:281
  (70 shorter events, 10.0 us)
Async XLA Ops:
  2.0 12.6 %collective-permute-start.9 = (bf16[1536,128]{1,0:T(8,128)(2,1)S(1)}, bf16[1536,128]{1,0:T(8,128)(2,1)S(1)}, u32[]{:S(2)}, u32[]{:S(2)}) collective-permute-start(bf16[1536,128]{1,0:T(8,128)(2,1)S(1)} %get-tuple-element.48), channel_id=1, source_target_pairs={{0,3},{1,0},{2,1},{3,2},{4,7},{5,4},{6,5},{7,6},{8,11},{9,8},{10,9... | collective-permute-start | bytes 1179656 | tf_op jit(solution)/shard_map/ppermute | solution.py:46
  5.6 12.3 %collective-permute-start.8 = (bf16[1536,128]{1,0:T(8,128)(2,1)S(1)}, bf16[1536,128]{1,0:T(8,128)(2,1)S(1)}, u32[]{:S(2)}, u32[]{:S(2)}) collective-permute-start(bf16[1536,128]{1,0:T(8,128)(2,1)S(1)} %get-tuple-element.48), channel_id=1, source_target_pairs={{0,1},{1,2},{2,3},{3,0},{4,5},{5,6},{6,7},{7,4},{8,9},{9,10},{10,1... | collective-permute-start | bytes 1179656 | tf_op jit(solution)/shard_map/ppermute | solution.py:46
  5.6 12.3 %collective-permute-start.10 = (bf16[1536,128]{1,0:T(8,128)(2,1)S(1)}, bf16[1536,128]{1,0:T(8,128)(2,1)S(1)}, u32[]{:S(2)}, u32[]{:S(2)}) collective-permute-start(bf16[1536,128]{1,0:T(8,128)(2,1)S(1)} %get-tuple-element.48), channel_id=1, source_target_pairs={{0,2},{1,3},{2,0},{3,1},{4,6},{5,7},{6,4},{7,5},{8,10},{9,11},{10,... | collective-permute-start | bytes 1179656 | tf_op jit(solution)/shard_map/ppermute | solution.py:46
  7.2 13.5 %collective-permute-start.1 = (bf16[1536,128]{1,0:T(8,128)(2,1)S(1)}, bf16[1536,128]{1,0:T(8,128)(2,1)S(1)}, u32[]{:S(2)}, u32[]{:S(2)}) collective-permute-start(bf16[1536,128]{1,0:T(8,128)(2,1)S(1)} %get-tuple-element.49), channel_id=1, source_target_pairs={{0,3},{1,0},{2,1},{3,2},{4,7},{5,4},{6,5},{7,6},{8,11},{9,8},{10,9... | collective-permute-start | bytes 1179656 | tf_op jit(solution)/shard_map/ppermute | solution.py:46
  8.3 18.1 %collective-permute-start = (bf16[1536,128]{1,0:T(8,128)(2,1)S(1)}, bf16[1536,128]{1,0:T(8,128)(2,1)S(1)}, u32[]{:S(2)}, u32[]{:S(2)}) collective-permute-start(bf16[1536,128]{1,0:T(8,128)(2,1)S(1)} %get-tuple-element.49), channel_id=1, source_target_pairs={{0,1},{1,2},{2,3},{3,0},{4,5},{5,6},{6,7},{7,4},{8,9},{9,10},{10,1... | collective-permute-start | bytes 1179656 | tf_op jit(solution)/shard_map/ppermute | solution.py:46
  14.5 11.8 %collective-permute-start.2 = (bf16[1536,128]{1,0:T(8,128)(2,1)S(1)}, bf16[1536,128]{1,0:T(8,128)(2,1)S(1)}, u32[]{:S(2)}, u32[]{:S(2)}) collective-permute-start(bf16[1536,128]{1,0:T(8,128)(2,1)S(1)} %get-tuple-element.49), channel_id=1, source_target_pairs={{0,2},{1,3},{2,0},{3,1},{4,6},{5,7},{6,4},{7,5},{8,10},{9,11},{10,... | collective-permute-start | bytes 1179656 | tf_op jit(solution)/shard_map/ppermute | solution.py:46
  18.1 61.7 %copy-start = (bf16[4,1536,128]{2,1,0:T(8,128)(2,1)}, bf16[4,1536,128]{2,1,0:T(8,128)(2,1)S(1)}, u32[]{:S(2)}) copy-start(bf16[4,1536,128]{2,1,0:T(8,128)(2,1)S(1)} %pad_maximum_fusion.1.refs_1_.refs_6_) | copy-start | bytes 4718596
  18.2 12.0 %copy-start.2 = (bf16[1536,512]{1,0:T(8,128)(2,1)S(1)}, bf16[1536,512]{1,0:T(8,128)(2,1)}, u32[]{:S(2)}) copy-start(bf16[1536,512]{1,0:T(8,128)(2,1)} %hidden.1) | copy-start | bytes 4718596
  18.2 11.9 %copy-start.4 = (bf16[1536,512]{1,0:T(8,128)(2,1)S(1)}, bf16[1536,512]{1,0:T(8,128)(2,1)}, u32[]{:S(2)}) copy-start(bf16[1536,512]{1,0:T(8,128)(2,1)} %gate.1) | copy-start | bytes 4718596
  18.2 46.4 %collective-permute-start.12 = (bf16[4,1536,128]{2,1,0:T(8,128)(2,1)S(1)}, bf16[4,1536,128]{2,1,0:T(8,128)(2,1)}, u32[]{:S(2)}, u32[]{:S(2)}) collective-permute-start(bf16[4,1536,128]{2,1,0:T(8,128)(2,1)S(1)} %pad_maximum_fusion.1.refs_1_.refs_6_), channel_id=1, source_target_pairs={{0,12},{1,13},{2,14},{3,15},{4,0},{5,1},{6,2},{7,3},{8,4},{9,5},{1... | collective-permute-start | bytes 4718600 | tf_op jit(solution)/shard_map/ppermute | solution.py:46
  20.7 45.5 %collective-permute-start.11 = (bf16[4,1536,128]{2,1,0:T(8,128)(2,1)S(1)}, bf16[4,1536,128]{2,1,0:T(8,128)(2,1)}, u32[]{:S(2)}, u32[]{:S(2)}) collective-permute-start(bf16[4,1536,128]{2,1,0:T(8,128)(2,1)S(1)} %pad_maximum_fusion.1.refs_1_.refs_6_), channel_id=1, source_target_pairs={{0,4},{1,5},{2,6},{3,7},{4,8},{5,9},{6,10},{7,11},{8,12},{9,13},{1... | collective-permute-start | bytes 4718600 | tf_op jit(solution)/shard_map/ppermute | solution.py:46
  26.6 45.7 %collective-permute-start.4 = (bf16[4,1536,128]{2,1,0:T(8,128)(2,1)S(1)}, bf16[4,1536,128]{2,1,0:T(8,128)(2,1)}, u32[]{:S(2)}, u32[]{:S(2)}) collective-permute-start(bf16[4,1536,128]{2,1,0:T(8,128)(2,1)S(1)} %pad_maximum_fusion.refs_1_), channel_id=1, source_target_pairs={{0,12},{1,13},{2,14},{3,15},{4,0},{5,1},{6,2},{7,3},{8,4},{9,5},{1... | collective-permute-start | bytes 4718600 | tf_op jit(solution)/shard_map/ppermute | solution.py:46
  30.1 44.6 %collective-permute-start.3 = (bf16[4,1536,128]{2,1,0:T(8,128)(2,1)S(1)}, bf16[4,1536,128]{2,1,0:T(8,128)(2,1)}, u32[]{:S(2)}, u32[]{:S(2)}) collective-permute-start(bf16[4,1536,128]{2,1,0:T(8,128)(2,1)S(1)} %pad_maximum_fusion.refs_1_), channel_id=1, source_target_pairs={{0,4},{1,5},{2,6},{3,7},{4,8},{5,9},{6,10},{7,11},{8,12},{9,13},{1... | collective-permute-start | bytes 4718600 | tf_op jit(solution)/shard_map/ppermute | solution.py:46
  31.9 32.6 %all-to-all-start = ((f32[16,1,1536]{2,1,0:T(1,128)}), f32[16,1,1536]{2,1,0:T(1,128)S(1)}, u32[]{:S(2)}, u32[]{:S(2)}) async-start(f32[16,1,1536]{2,1,0:T(1,128)} %broadcast_in_dim.8), calls=%async_computation | async-start | bytes 196608 | tf_op jit(solution)/shard_map/all_to_all | solution.py:254
  39.5 29.4 %copy-start.1 = (f32[512]{0:T(512)S(1)}, f32[512]{0:T(512)}, u32[]{:S(2)}) copy-start(f32[512]{0:T(512)} %param.7) | copy-start | bytes 6148
  65.9 11.4 %collective-permute-start.14 = (bf16[2,1536,128]{2,1,0:T(8,128)(2,1)S(1)}, bf16[2,1536,128]{2,1,0:T(8,128)(2,1)S(1)}, u32[]{:S(2)}, u32[]{:S(2)}) collective-permute-start(bf16[2,1536,128]{2,1,0:T(8,128)(2,1)S(1)} %slice.48), channel_id=1, source_target_pairs={{0,12},{1,13},{2,14},{3,15},{4,0},{5,1},{6,2},{7,3},{8,4},{9,5},{1... | collective-permute-start | bytes 2359304 | tf_op jit(solution)/shard_map/ppermute | solution.py:46
  67.4 12.4 %collective-permute-start.13 = (bf16[2,1536,128]{2,1,0:T(8,128)(2,1)S(1)}, bf16[2,1536,128]{2,1,0:T(8,128)(2,1)S(1)}, u32[]{:S(2)}, u32[]{:S(2)}) collective-permute-start(bf16[2,1536,128]{2,1,0:T(8,128)(2,1)S(1)} %slice.47), channel_id=1, source_target_pairs={{0,4},{1,5},{2,6},{3,7},{4,8},{5,9},{6,10},{7,11},{8,12},{9,13},{1... | collective-permute-start | bytes 2359304 | tf_op jit(solution)/shard_map/ppermute | solution.py:46
  73.4 14.1 %collective-permute-start.6 = (bf16[2,1536,128]{2,1,0:T(8,128)(2,1)S(1)}, bf16[2,1536,128]{2,1,0:T(8,128)(2,1)S(1)}, u32[]{:S(2)}, u32[]{:S(2)}) collective-permute-start(bf16[2,1536,128]{2,1,0:T(8,128)(2,1)S(1)} %slice.45), channel_id=1, source_target_pairs={{0,12},{1,13},{2,14},{3,15},{4,0},{5,1},{6,2},{7,3},{8,4},{9,5},{1... | collective-permute-start | bytes 2359304 | tf_op jit(solution)/shard_map/ppermute | solution.py:46
  75.9 12.1 %collective-permute-start.5 = (bf16[2,1536,128]{2,1,0:T(8,128)(2,1)S(1)}, bf16[2,1536,128]{2,1,0:T(8,128)(2,1)S(1)}, u32[]{:S(2)}, u32[]{:S(2)}) collective-permute-start(bf16[2,1536,128]{2,1,0:T(8,128)(2,1)S(1)} %slice.44), channel_id=1, source_target_pairs={{0,4},{1,5},{2,6},{3,7},{4,8},{5,9},{6,10},{7,11},{8,12},{9,13},{1... | collective-permute-start | bytes 2359304 | tf_op jit(solution)/shard_map/ppermute | solution.py:46
  87.4 8.4 %copy-start.6 = (f32[1024,512]{1,0:T(8,128)S(1)}, f32[1024,512]{1,0:T(8,128)}, u32[]{:S(2)}) copy-start(f32[1024,512]{1,0:T(8,128)} %get-tuple-element.26.mine2) | copy-start | bytes 6291460
  87.4 8.3 %collective-permute-start.15 = (f32[1024,512]{1,0:T(8,128)}, f32[1024,512]{1,0:T(8,128)S(1)}, u32[]{:S(2)}, u32[]{:S(2)}) collective-permute-start(f32[1024,512]{1,0:T(8,128)} %get-tuple-element.27), channel_id=1, source_target_pairs={{0,16},{1,17},{2,18},{3,19},{4,20},{5,21},{6,22},{7,23},{8,24},{9,... | collective-permute-start | bytes 6291464 | tf_op jit(solution)/shard_map/ppermute | solution.py:46
  95.7 4.5 %collective-permute-start.7 = (f32[1024,512]{1,0:T(8,128)}, f32[1024,512]{1,0:T(8,128)S(1)}, u32[]{:S(2)}, u32[]{:S(2)}) collective-permute-start(f32[1024,512]{1,0:T(8,128)} %get-tuple-element.25), channel_id=1, source_target_pairs={{0,16},{1,17},{2,18},{3,19},{4,20},{5,21},{6,22},{7,23},{8,24},{9,... | collective-permute-start | bytes 6291464 | tf_op jit(solution)/shard_map/ppermute | solution.py:46
  95.8 4.6 %copy-start.7 = (f32[1024,512]{1,0:T(8,128)}, f32[1024,512]{1,0:T(8,128)S(1)}, u32[]{:S(2)}) copy-start(f32[1024,512]{1,0:T(8,128)S(1)} %collective-permute-done.15.came2) | copy-start | bytes 6291460
  100.1 18.0 %copy-start.9 = (f32[1024,512]{1,0:T(8,128)}, f32[1024,512]{1,0:T(8,128)S(1)}, u32[]{:S(2)}) copy-start(f32[1024,512]{1,0:T(8,128)S(1)} %collective-permute-done.7.came1) | copy-start | bytes 6291460
  100.4 17.8 %collective-permute-start.16 = (bf16[512,512]{1,0:T(8,128)(2,1)S(1)}, bf16[512,512]{1,0:T(8,128)(2,1)S(1)}, u32[]{:S(2)}, u32[]{:S(2)}) collective-permute-start(bf16[512,512]{1,0:T(8,128)(2,1)S(1)} %fusion.5), channel_id=1, source_target_pairs={{0,32},{1,33},{2,34},{3,35},{4,36},{5,37},{6,38},{7,39},{8,40},{9,... | collective-permute-start | bytes 1572872 | tf_op jit(solution)/shard_map/ppermute | solution.py:46
  106.2 12.2 %collective-permute-start.17 = (bf16[512,512]{1,0:T(8,128)(2,1)S(1)}, bf16[512,512]{1,0:T(8,128)(2,1)S(1)}, u32[]{:S(2)}, u32[]{:S(2)}) collective-permute-start(bf16[512,512]{1,0:T(8,128)(2,1)S(1)} %fusion.4), channel_id=1, source_target_pairs={{0,32},{1,33},{2,34},{3,35},{4,36},{5,37},{6,38},{7,39},{8,40},{9,... | collective-permute-start | bytes 1572872 | tf_op jit(solution)/shard_map/ppermute | solution.py:46
  122.8 33.7 %collective-permute-start.18 = (bf16[256,512]{1,0:T(8,128)(2,1)}, bf16[256,512]{1,0:T(8,128)(2,1)S(1)}, u32[]{:S(2)}, u32[]{:S(2)}) collective-permute-start(bf16[256,512]{1,0:T(8,128)(2,1)} %get-tuple-element.39), channel_id=1, source_target_pairs={{0,64},{1,65},{2,66},{3,67},{4,68},{5,69},{6,70},{7,71},{8,72},{9,... | collective-permute-start | bytes 786440 | tf_op jit(solution)/shard_map/ppermute | solution.py:46
  122.8 33.7 %collective-permute-start.19 = (bf16[256,512]{1,0:T(8,128)(2,1)}, bf16[256,512]{1,0:T(8,128)(2,1)S(1)}, u32[]{:S(2)}, u32[]{:S(2)}) collective-permute-start(bf16[256,512]{1,0:T(8,128)(2,1)} %get-tuple-element.40), channel_id=1, source_target_pairs={{0,192},{1,193},{2,194},{3,195},{4,196},{5,197},{6,198},{7,199},{8... | collective-permute-start | bytes 786440 | tf_op jit(solution)/shard_map/ppermute | solution.py:46
  126.4 30.1 %collective-permute-start.20 = (bf16[256,512]{1,0:T(8,128)(2,1)}, bf16[256,512]{1,0:T(8,128)(2,1)S(1)}, u32[]{:S(2)}, u32[]{:S(2)}) collective-permute-start(bf16[256,512]{1,0:T(8,128)(2,1)} %get-tuple-element.41), channel_id=1, source_target_pairs={{0,128},{1,129},{2,130},{3,131},{4,132},{5,133},{6,134},{7,135},{8... | collective-permute-start | bytes 786440 | tf_op jit(solution)/shard_map/ppermute | solution.py:46
  131.2 10.3 %all-to-all-start.1 = ((f32[16,1,1536]{2,1,0:T(1,128)}), f32[16,1,1536]{2,1,0:T(1,128)S(1)}, u32[]{:S(2)}, u32[]{:S(2)}) async-start(f32[16,1,1536]{2,1,0:T(1,128)} %broadcast_in_dim.10), calls=%async_computation.1 | async-start | bytes 196608 | tf_op jit(solution)/shard_map/all_to_all | solution.py:254
  142.8 13.1 %all-to-all-start.2 = ((f32[16,1,512]{2,1,0:T(1,128)}), f32[16,1,512]{2,1,0:T(1,128)S(1)}, u32[]{:S(2)}, u32[]{:S(2)}) async-start(f32[16,1,512]{2,1,0:T(1,128)} %broadcast_in_dim.11), calls=%async_computation.2 | async-start | bytes 65536 | tf_op jit(solution)/shard_map/all_to_all | solution.py:254
  148.7 7.9 %copy-start.10 = (f32[256,512]{1,0:T(8,128)S(1)}, f32[256,512]{1,0:T(8,128)}, u32[]{:S(2)}) copy-start(f32[256,512]{1,0:T(8,128)} %get-tuple-element.38) | copy-start | bytes 1572868
  (5 other events, 15.0 us)
where the time goes:
time: 158 us; the launch traced here: 157 us
  waiting for transfers between devices  53.9 us (34%)
  starting transfers between devices  45 us (28%)
  Pallas kernels  37.8 us (24%)
  local copies, waits for them, and re-layouts  10.4 us (7%)
  other arithmetic  6.93 us (4%)
  between operations  3.4 us (2%)
    all_to_all x3, waiting for transfers between devices, parts_of(): return lax.all_to_all(spread, axis, 0, 0, tiled=True)  30.8 us
    ppermute x21, starting transfers between devices, send(): return lax.ppermute(value, AXES, table)  30.2 us
    pallas_call x3, Pallas kernels, block_kernel(): pl.pallas_call(lambda *refs: block_body(groups, len(stacks), has_acc, las...  27 us
    ppermute x21, waiting for transfers between devices, send(): return lax.ppermute(value, AXES, table)  23.1 us
    all_to_all x3, starting transfers between devices, parts_of(): return lax.all_to_all(spread, axis, 0, 0, tiled=True)  14.8 us
    pallas_call x1, Pallas kernels, last(): pl.pallas_call(last_body, grid=(tok // tile,), out_shape=(jax.ShapeDtypeS...  7.21 us
    pallas_call x1, Pallas kernels, mix(): pl.pallas_call(mix_body, grid=(1,), out_shape=(jax.ShapeDtypeStruct((2 *...  3.65 us
    convert_element_type x1, other arithmetic, local(): normed = (normalized * norm_weight).astype(BF)  3.28 us
  transfers between devices with their start and end apart: 24, of which 10 were waited for; matrix products, arithmetic and copies ran while one was open for 9% of the time, Pallas kernels for 22%

commit v1 on v0

--- a/solution.py
+++ b/solution.py
@@ -349,15 +349,18 @@
     )
     got1, got2, stat = lax.optimization_barrier((got1, got2, stat))
     own, *outs = mix(mine1, came1, got1, mine2, came2, got2)
-    rows = own
-    for block, d in zip((outs[1], outs[2], outs[0]), (2, -2, 4)):
-        rows = rows + send(block, along_z(d)).astype(F32)
-    products = parts_of(stat, "tensor")
+    gots = [send(block, along_z(d)) for block, d in zip((outs[1], outs[2], outs[0]), (2, -2, 4))]
+    products = parts_of(jnp.tile(stat, (1, 4)), "tensor")
     grad_hidden, grad_gate = last(
         hidden_states, gate_values, grad_normed, normalized, norm_weight[None], inverse_rms[None], products
     )
     gain, _ = lax.optimization_barrier((gain[0], products))
-    grad_norm_weight = total(gain, "seq")
+    gains = parts_of(gain, "seq")
+    gains, gots = lax.optimization_barrier((gains, gots))
+    grad_norm_weight = jnp.sum(gains, axis=0)
+    rows = own
+    for got in gots:
+        rows = rows + got.astype(F32)
     return grad_hidden, grad_gate, rows, grad_norm_weight
 
 

time: 158 us -> 159 us (level); the launches traced: 157 us -> 157 us
  transfers between devices with their start and end apart: 24 -> 24, of which waited for: 10 -> 10; matrix products, arithmetic and copies ran while one was open for 9% -> 8% of each run, Pallas kernels for 22% -> 24%
where the time goes in v1:
time: 159 us; the launch traced here: 157 us
  waiting for transfers between devices  53.2 us (33%)
  starting transfers between devices  45.1 us (28%)
  Pallas kernels  37.8 us (24%)
  local copies, waits for them, and re-layouts  10.1 us (6%)
  other arithmetic  6.91 us (4%)
  between operations  3.42 us (2%)
    ppermute x21, starting transfers between devices, send(): return lax.ppermute(value, AXES, table)  30.2 us
    all_to_all x3, waiting for transfers between devices, parts_of(): return lax.all_to_all(spread, axis, 0, 0, tiled=True)  30.1 us
    pallas_call x3, Pallas kernels, block_kernel(): pl.pallas_call(lambda *refs: block_body(groups, len(stacks), has_acc, las...  27 us
    ppermute x21, waiting for transfers between devices, send(): return lax.ppermute(value, AXES, table)  23.1 us
    all_to_all x3, starting transfers between devices, parts_of(): return lax.all_to_all(spread, axis, 0, 0, tiled=True)  14.9 us
    pallas_call x1, Pallas kernels, last(): pl.pallas_call(last_body, grid=(tok // tile,), out_shape=(jax.ShapeDtypeS...  7.19 us
    pallas_call x1, Pallas kernels, mix(): pl.pallas_call(mix_body, grid=(1,), out_shape=(jax.ShapeDtypeStruct((2 *...  3.65 us
    convert_element_type x1, other arithmetic, local(): normed = (normalized * norm_weight).astype(BF)  3.28 us
  transfers between devices with their start and end apart: 24, of which 10 were waited for; matrix products, arithmetic and copies ran while one was open for 8% of the time, Pallas kernels for 24%

profile of v1, /device:TPU:1, one launch (start us, length us, event | category | flops | bytes accessed | tf_op | source)
XLA Modules:
  0.0 156.6 jit_solution(15612661639997381673)
XLA Ops:
  0.6 1.3 slice_bitcast_fusion
  2.0 3.6 %collective-permute-start.9 = (bf16[1536,128]{1,0:T(8,128)(2,1)S(1)}, bf16[1536,128]{1,0:T(8,128)(2,1)S(1)}, u32[]{:S(2)}, u32[]{:S(2)}) collective-permute-start(bf16[1536,128]{1,0:T(8,128)(2,1)S(1)} %get-tuple-element.56), channel_id=1, source_target_pairs={{0,3},{1,0},{2,1},{3,2},{4,7},{5,4},{6,5},{7,6},{8,11},{9,8},{10,9... | collective-permute-start | bytes 1179656 | tf_op jit(solution)/shard_map/ppermute | solution.py:46
  5.6 1.6 %collective-permute-start.10 = (bf16[1536,128]{1,0:T(8,128)(2,1)S(1)}, bf16[1536,128]{1,0:T(8,128)(2,1)S(1)}, u32[]{:S(2)}, u32[]{:S(2)}) collective-permute-start(bf16[1536,128]{1,0:T(8,128)(2,1)S(1)} %get-tuple-element.56), channel_id=1, source_target_pairs={{0,2},{1,3},{2,0},{3,1},{4,6},{5,7},{6,4},{7,5},{8,10},{9,11},{10,... | collective-permute-start | bytes 1179656 | tf_op jit(solution)/shard_map/ppermute | solution.py:46
  8.9 5.7 %collective-permute-done.9 = bf16[1536,128]{1,0:T(8,128)(2,1)S(1)} collective-permute-done((bf16[1536,128]{1,0:T(8,128)(2,1)S(1)}, bf16[1536,128]{1,0:T(8,128)(2,1)S(1)}, u32[]{:S(2)}, u32[]{:S(2)}) %collective-permute-start.9) | collective-permute-done | bytes 393248 | tf_op jit(solution)/shard_map/ppermute | solution.py:46
  14.5 3.4 %collective-permute-done.8 = bf16[1536,128]{1,0:T(8,128)(2,1)S(1)} collective-permute-done((bf16[1536,128]{1,0:T(8,128)(2,1)S(1)}, bf16[1536,128]{1,0:T(8,128)(2,1)S(1)}, u32[]{:S(2)}, u32[]{:S(2)}) %collective-permute-start.8) | collective-permute-done | bytes 393248 | tf_op jit(solution)/shard_map/ppermute | solution.py:46
  18.2 2.6 %collective-permute-start.12 = (bf16[4,1536,128]{2,1,0:T(8,128)(2,1)S(1)}, bf16[4,1536,128]{2,1,0:T(8,128)(2,1)}, u32[]{:S(2)}, u32[]{:S(2)}) collective-permute-start(bf16[4,1536,128]{2,1,0:T(8,128)(2,1)S(1)} %pad_maximum_fusion.1.refs_1_.refs_6_), channel_id=1, source_target_pairs={{0,12},{1,13},{2,14},{3,15},{4,0},{5,1},{6,2},{7,3},{8,4},{9,5},{1... | collective-permute-start | bytes 4718600 | tf_op jit(solution)/shard_map/ppermute | solution.py:46
  20.7 5.6 %collective-permute-done = bf16[1536,128]{1,0:T(8,128)(2,1)S(1)} collective-permute-done((bf16[1536,128]{1,0:T(8,128)(2,1)S(1)}, bf16[1536,128]{1,0:T(8,128)(2,1)S(1)}, u32[]{:S(2)}, u32[]{:S(2)}) %collective-permute-start) | collective-permute-done | bytes 393248 | tf_op jit(solution)/shard_map/ppermute | solution.py:46
  26.6 3.5 %collective-permute-start.4 = (bf16[4,1536,128]{2,1,0:T(8,128)(2,1)S(1)}, bf16[4,1536,128]{2,1,0:T(8,128)(2,1)}, u32[]{:S(2)}, u32[]{:S(2)}) collective-permute-start(bf16[4,1536,128]{2,1,0:T(8,128)(2,1)S(1)} %pad_maximum_fusion.refs_1_), channel_id=1, source_target_pairs={{0,12},{1,13},{2,14},{3,15},{4,0},{5,1},{6,2},{7,3},{8,4},{9,5},{1... | collective-permute-start | bytes 4718600 | tf_op jit(solution)/shard_map/ppermute | solution.py:46
  30.1 1.1 multiply_reduce_fusion
  31.9 6.0 %all-to-all-start = ((f32[16,1,1536]{2,1,0:T(1,128)}), f32[16,1,1536]{2,1,0:T(1,128)S(1)}, u32[]{:S(2)}, u32[]{:S(2)}) async-start(f32[16,1,1536]{2,1,0:T(1,128)} %broadcast_in_dim.8), calls=%async_computation | async-start | bytes 196608 | tf_op jit(solution)/shard_map/all_to_all | solution.py:254
  40.5 24.0 %all-to-all-done = f32[16,1,1536]{2,1,0:T(1,128)S(1)} async-done(((f32[16,1,1536]{2,1,0:T(1,128)}), f32[16,1,1536]{2,1,0:T(1,128)S(1)}, u32[]{:S(2)}, u32[]{:S(2)}) %all-to-all-start) | async-done | bytes 98336 | tf_op jit(solution)/shard_map/all_to_all | solution.py:254
  64.6 1.3 slice.48
  66.2 1.2 slice.47
  67.4 1.5 collective-permute-start.13
  69.0 3.3 %multiply_convert_fusion = (bf16[1536,512]{1,0:T(8,128)(2,1)}, f32[1536,512]{1,0:T(8,128)}) fusion(f32[512]{0:T(512)S(1)} %copy-done.1, f32[1536]{0:T(1024)S(1)} %add_rsqrt_fusion, bf16[1536,512]{1,0:T(8,128)(2,1)S(1)} %copy-done.5, bf16[1536,512]{1,0:T(8,128)(2,1)S(1)} %copy-done.3), kind=kLoop, calls=%fused_computation.6 | loop fusion | flops 7864320 | bytes 7872512 | tf_op jit(solution)/shard_map/convert_element_type | solution.py:330
  72.2 1.2 slice.45
  73.4 1.3 collective-permute-start.6
  74.7 1.2 slice.44
  76.2 1.1 collective-permute-done.14.refs_5_.refs_10_
  77.3 2.5 %collective-permute-done.13.refs_4_.refs_9_ = bf16[2,1536,128]{2,1,0:T(8,128)(2,1)S(1)} collective-permute-done((bf16[2,1536,128]{2,1,0:T(8,128)(2,1)S(1)}, bf16[2,1536,128]{2,1,0:T(8,128)(2,1)S(1)}, u32[]{:S(2)}, u32[]{:S(2)}) %collective-permute-start.13) | collective-permute-done | bytes 786464 | tf_op jit(solution)/shard_map/ppermute | solution.py:46
  79.8 7.6 %outer2.1 = (f32[1024,512]{1,0:T(8,128)}, f32[1024,512]{1,0:T(8,128)}) custom-call(s32[32]{0:T(128)S(1)} %stack.161.refs_0_, bf16[4,1536,128]{2,1,0:T(8,128)(2,1)S(1)} %pad_maximum_fusion.1.refs_1_.refs_6_, bf16[4,1536,128]{2,1,0:T(8,128)(2,1)} %collective-permute-done.11.refs_2_.refs_7_, bf16[4,1536,128]{2,1,0:T(8,128)(2,1)} %collective-permute-done.12.refs_3_.refs_8_, ...), custom_call_target="tpu_custom_call" | custom-call | flops 32000000000 | bytes 96000000 | tf_op jit(solution)/shard_map/outer2/pallas_call | solution.py:217
  88.1 7.6 %outer1.1 = (f32[1024,512]{1,0:T(8,128)}, f32[1024,512]{1,0:T(8,128)}) custom-call(s32[32]{0:T(128)S(1)} %stack.161.refs_0_, bf16[4,1536,128]{2,1,0:T(8,128)(2,1)S(1)} %pad_maximum_fusion.refs_1_, bf16[4,1536,128]{2,1,0:T(8,128)(2,1)} %collective-permute-done.3.refs_2_, bf16[4,1536,128]{2,1,0:T(8,128)(2,1)} %collective-permute-done.4.refs_3_, ...), custom_call_target="tpu_custom_call" | custom-call | flops 32000000000 | bytes 96000000 | tf_op jit(solution)/shard_map/outer1/pallas_call | solution.py:217
  96.0 4.1 %collective-permute-done.7.came1 = f32[1024,512]{1,0:T(8,128)S(1)} collective-permute-done((f32[1024,512]{1,0:T(8,128)}, f32[1024,512]{1,0:T(8,128)S(1)}, u32[]{:S(2)}, u32[]{:S(2)}) %collective-permute-start.7) | collective-permute-done | bytes 2097184 | tf_op jit(solution)/shard_map/ppermute | solution.py:46
  100.4 5.8 %collective-permute-start.16 = (bf16[512,512]{1,0:T(8,128)(2,1)S(1)}, bf16[512,512]{1,0:T(8,128)(2,1)S(1)}, u32[]{:S(2)}, u32[]{:S(2)}) collective-permute-start(bf16[512,512]{1,0:T(8,128)(2,1)S(1)} %fusion.5), channel_id=1, source_target_pairs={{0,32},{1,33},{2,34},{3,35},{4,36},{5,37},{6,38},{7,39},{8,40},{9,... | collective-permute-start | bytes 1572872 | tf_op jit(solution)/shard_map/ppermute | solution.py:46
  106.3 11.8 %inner.1 = (f32[1536,512]{1,0:T(8,128)}, f32[1,1536]{1,0:T(1,128)S(1)}, f32[8,512]{1,0:T(8,128)S(1)}) custom-call(s32[32]{0:T(128)S(1)} %stack.161.refs_0_, bf16[4,1536,128]{2,1,0:T(8,128)(2,1)S(1)} %pad_maximum_fusion.refs_1_, bf16[4,1536,128]{2,1,0:T(8,128)(2,1)} %collective-permute-done.3.refs_2_, bf16[4,1536,128]{2,1,0:T(8,128)(2,1)} %collective-permute-done.4.refs_3_, ...), custom_call_target="tpu_custom_call" | custom-call | flops 64000000000 | bytes 192000000 | tf_op jit(solution)/shard_map/inner/pallas_call | solution.py:217
  119.4 3.6 %all-to-all-start.1 = ((f32[16,1,6144]{2,1,0:T(1,128)}), f32[16,1,6144]{2,1,0:T(1,128)S(1)}, u32[]{:S(2)}, u32[]{:S(2)}) async-start(f32[16,1,6144]{2,1,0:T(1,128)} %broadcast_in_dim.10), calls=%async_computation.1 | async-start | bytes 786432 | tf_op jit(solution)/shard_map/all_to_all | solution.py:254
  123.0 3.7 %mix.1 = (f32[256,512]{1,0:T(8,128)}, bf16[256,512]{1,0:T(8,128)(2,1)}, bf16[256,512]{1,0:T(8,128)(2,1)}, bf16[256,512]{1,0:T(8,128)(2,1)}) custom-call(f32[1024,512]{1,0:T(8,128)} %get-tuple-element.28.mine1, f32[1024,512]{1,0:T(8,128)} %copy-done.9, bf16[512,512]{1,0:T(8,128)(2,1)} %copy-done.11, f32[1024,512]{1,0:T(8,128)} %get-tuple-element.30.mine2, ...), custom_call_target="tpu_custom_call" | custom-call | flops 4000000 | bytes 8000000 | tf_op jit(solution)/shard_map/mix/pallas_call | solution.py:241
  126.6 3.6 %collective-permute-start.19 = (bf16[256,512]{1,0:T(8,128)(2,1)}, bf16[256,512]{1,0:T(8,128)(2,1)S(1)}, u32[]{:S(2)}, u32[]{:S(2)}) collective-permute-start(bf16[256,512]{1,0:T(8,128)(2,1)} %get-tuple-element.46), channel_id=1, source_target_pairs={{0,192},{1,193},{2,194},{3,195},{4,196},{5,197},{6,198},{7,199},{8... | collective-permute-start | bytes 786440 | tf_op jit(solution)/shard_map/ppermute | solution.py:46
  130.2 4.1 %collective-permute-start.20 = (bf16[256,512]{1,0:T(8,128)(2,1)}, bf16[256,512]{1,0:T(8,128)(2,1)S(1)}, u32[]{:S(2)}, u32[]{:S(2)}) collective-permute-start(bf16[256,512]{1,0:T(8,128)(2,1)} %get-tuple-element.47), channel_id=1, source_target_pairs={{0,128},{1,129},{2,130},{3,131},{4,132},{5,133},{6,134},{7,135},{8... | collective-permute-start | bytes 786440 | tf_op jit(solution)/shard_map/ppermute | solution.py:46
  135.8 5.3 %all-to-all-start.2 = ((f32[16,1,512]{2,1,0:T(1,128)}), f32[16,1,512]{2,1,0:T(1,128)S(1)}, u32[]{:S(2)}, u32[]{:S(2)}) async-start(f32[16,1,512]{2,1,0:T(1,128)} %broadcast_in_dim.11), calls=%async_computation.2 | async-start | bytes 65536 | tf_op jit(solution)/shard_map/all_to_all | solution.py:254
  141.8 7.2 %last.1 = (bf16[1536,512]{1,0:T(8,128)(2,1)}, bf16[1536,512]{1,0:T(8,128)(2,1)}) custom-call(bf16[1536,512]{1,0:T(8,128)(2,1)} %hidden.1, bf16[1536,512]{1,0:T(8,128)(2,1)} %gate.1, f32[1536,512]{1,0:T(8,128)} %get-tuple-element.33.grad, f32[1536,512]{1,0:T(8,128)} %get-tuple-element.53.refs_13_.normalized, f32[1,512]{1,0:T(1,128)} %bitcast.50, ...), custom_call_target="tpu_custom_call" | custom-call | flops 1000 | bytes 1000 | tf_op jit(solution)/shard_map/last/pallas_call | solution.py:281
  149.0 6.1 %all-to-all-done.2 = f32[16,1,512]{2,1,0:T(1,128)S(1)} async-done(((f32[16,1,512]{2,1,0:T(1,128)}), f32[16,1,512]{2,1,0:T(1,128)S(1)}, u32[]{:S(2)}, u32[]{:S(2)}) %all-to-all-start.2) | async-done | bytes 32800 | tf_op jit(solution)/shard_map/all_to_all | solution.py:254
  (73 shorter events, 9.7 us)
Async XLA Ops:
  2.0 12.6 %collective-permute-start.9 = (bf16[1536,128]{1,0:T(8,128)(2,1)S(1)}, bf16[1536,128]{1,0:T(8,128)(2,1)S(1)}, u32[]{:S(2)}, u32[]{:S(2)}) collective-permute-start(bf16[1536,128]{1,0:T(8,128)(2,1)S(1)} %get-tuple-element.56), channel_id=1, source_target_pairs={{0,3},{1,0},{2,1},{3,2},{4,7},{5,4},{6,5},{7,6},{8,11},{9,8},{10,9... | collective-permute-start | bytes 1179656 | tf_op jit(solution)/shard_map/ppermute | solution.py:46
  5.6 12.3 %collective-permute-start.8 = (bf16[1536,128]{1,0:T(8,128)(2,1)S(1)}, bf16[1536,128]{1,0:T(8,128)(2,1)S(1)}, u32[]{:S(2)}, u32[]{:S(2)}) collective-permute-start(bf16[1536,128]{1,0:T(8,128)(2,1)S(1)} %get-tuple-element.56), channel_id=1, source_target_pairs={{0,1},{1,2},{2,3},{3,0},{4,5},{5,6},{6,7},{7,4},{8,9},{9,10},{10,1... | collective-permute-start | bytes 1179656 | tf_op jit(solution)/shard_map/ppermute | solution.py:46
  5.6 12.3 %collective-permute-start.10 = (bf16[1536,128]{1,0:T(8,128)(2,1)S(1)}, bf16[1536,128]{1,0:T(8,128)(2,1)S(1)}, u32[]{:S(2)}, u32[]{:S(2)}) collective-permute-start(bf16[1536,128]{1,0:T(8,128)(2,1)S(1)} %get-tuple-element.56), channel_id=1, source_target_pairs={{0,2},{1,3},{2,0},{3,1},{4,6},{5,7},{6,4},{7,5},{8,10},{9,11},{10,... | collective-permute-start | bytes 1179656 | tf_op jit(solution)/shard_map/ppermute | solution.py:46
  7.2 13.5 %collective-permute-start.1 = (bf16[1536,128]{1,0:T(8,128)(2,1)S(1)}, bf16[1536,128]{1,0:T(8,128)(2,1)S(1)}, u32[]{:S(2)}, u32[]{:S(2)}) collective-permute-start(bf16[1536,128]{1,0:T(8,128)(2,1)S(1)} %get-tuple-element.57), channel_id=1, source_target_pairs={{0,3},{1,0},{2,1},{3,2},{4,7},{5,4},{6,5},{7,6},{8,11},{9,8},{10,9... | collective-permute-start | bytes 1179656 | tf_op jit(solution)/shard_map/ppermute | solution.py:46
  8.3 18.1 %collective-permute-start = (bf16[1536,128]{1,0:T(8,128)(2,1)S(1)}, bf16[1536,128]{1,0:T(8,128)(2,1)S(1)}, u32[]{:S(2)}, u32[]{:S(2)}) collective-permute-start(bf16[1536,128]{1,0:T(8,128)(2,1)S(1)} %get-tuple-element.57), channel_id=1, source_target_pairs={{0,1},{1,2},{2,3},{3,0},{4,5},{5,6},{6,7},{7,4},{8,9},{9,10},{10,1... | collective-permute-start | bytes 1179656 | tf_op jit(solution)/shard_map/ppermute | solution.py:46
  14.5 11.8 %collective-permute-start.2 = (bf16[1536,128]{1,0:T(8,128)(2,1)S(1)}, bf16[1536,128]{1,0:T(8,128)(2,1)S(1)}, u32[]{:S(2)}, u32[]{:S(2)}) collective-permute-start(bf16[1536,128]{1,0:T(8,128)(2,1)S(1)} %get-tuple-element.57), channel_id=1, source_target_pairs={{0,2},{1,3},{2,0},{3,1},{4,6},{5,7},{6,4},{7,5},{8,10},{9,11},{10,... | collective-permute-start | bytes 1179656 | tf_op jit(solution)/shard_map/ppermute | solution.py:46
  18.1 61.7 %copy-start = (bf16[4,1536,128]{2,1,0:T(8,128)(2,1)}, bf16[4,1536,128]{2,1,0:T(8,128)(2,1)S(1)}, u32[]{:S(2)}) copy-start(bf16[4,1536,128]{2,1,0:T(8,128)(2,1)S(1)} %pad_maximum_fusion.1.refs_1_.refs_6_) | copy-start | bytes 4718596
  18.2 12.0 %copy-start.2 = (bf16[1536,512]{1,0:T(8,128)(2,1)S(1)}, bf16[1536,512]{1,0:T(8,128)(2,1)}, u32[]{:S(2)}) copy-start(bf16[1536,512]{1,0:T(8,128)(2,1)} %hidden.1) | copy-start | bytes 4718596
  18.2 11.9 %copy-start.4 = (bf16[1536,512]{1,0:T(8,128)(2,1)S(1)}, bf16[1536,512]{1,0:T(8,128)(2,1)}, u32[]{:S(2)}) copy-start(bf16[1536,512]{1,0:T(8,128)(2,1)} %gate.1) | copy-start | bytes 4718596
  18.2 46.4 %collective-permute-start.12 = (bf16[4,1536,128]{2,1,0:T(8,128)(2,1)S(1)}, bf16[4,1536,128]{2,1,0:T(8,128)(2,1)}, u32[]{:S(2)}, u32[]{:S(2)}) collective-permute-start(bf16[4,1536,128]{2,1,0:T(8,128)(2,1)S(1)} %pad_maximum_fusion.1.refs_1_.refs_6_), channel_id=1, source_target_pairs={{0,12},{1,13},{2,14},{3,15},{4,0},{5,1},{6,2},{7,3},{8,4},{9,5},{1... | collective-permute-start | bytes 4718600 | tf_op jit(solution)/shard_map/ppermute | solution.py:46
  20.7 45.5 %collective-permute-start.11 = (bf16[4,1536,128]{2,1,0:T(8,128)(2,1)S(1)}, bf16[4,1536,128]{2,1,0:T(8,128)(2,1)}, u32[]{:S(2)}, u32[]{:S(2)}) collective-permute-start(bf16[4,1536,128]{2,1,0:T(8,128)(2,1)S(1)} %pad_maximum_fusion.1.refs_1_.refs_6_), channel_id=1, source_target_pairs={{0,4},{1,5},{2,6},{3,7},{4,8},{5,9},{6,10},{7,11},{8,12},{9,13},{1... | collective-permute-start | bytes 4718600 | tf_op jit(solution)/shard_map/ppermute | solution.py:46
  26.6 45.7 %collective-permute-start.4 = (bf16[4,1536,128]{2,1,0:T(8,128)(2,1)S(1)}, bf16[4,1536,128]{2,1,0:T(8,128)(2,1)}, u32[]{:S(2)}, u32[]{:S(2)}) collective-permute-start(bf16[4,1536,128]{2,1,0:T(8,128)(2,1)S(1)} %pad_maximum_fusion.refs_1_), channel_id=1, source_target_pairs={{0,12},{1,13},{2,14},{3,15},{4,0},{5,1},{6,2},{7,3},{8,4},{9,5},{1... | collective-permute-start | bytes 4718600 | tf_op jit(solution)/shard_map/ppermute | solution.py:46
  30.1 44.6 %collective-permute-start.3 = (bf16[4,1536,128]{2,1,0:T(8,128)(2,1)S(1)}, bf16[4,1536,128]{2,1,0:T(8,128)(2,1)}, u32[]{:S(2)}, u32[]{:S(2)}) collective-permute-start(bf16[4,1536,128]{2,1,0:T(8,128)(2,1)S(1)} %pad_maximum_fusion.refs_1_), channel_id=1, source_target_pairs={{0,4},{1,5},{2,6},{3,7},{4,8},{5,9},{6,10},{7,11},{8,12},{9,13},{1... | collective-permute-start | bytes 4718600 | tf_op jit(solution)/shard_map/ppermute | solution.py:46
  31.9 32.6 %all-to-all-start = ((f32[16,1,1536]{2,1,0:T(1,128)}), f32[16,1,1536]{2,1,0:T(1,128)S(1)}, u32[]{:S(2)}, u32[]{:S(2)}) async-start(f32[16,1,1536]{2,1,0:T(1,128)} %broadcast_in_dim.8), calls=%async_computation | async-start | bytes 196608 | tf_op jit(solution)/shard_map/all_to_all | solution.py:254
  39.5 29.4 %copy-start.1 = (f32[512]{0:T(512)S(1)}, f32[512]{0:T(512)}, u32[]{:S(2)}) copy-start(f32[512]{0:T(512)} %param.7) | copy-start | bytes 6148
  65.9 11.4 %collective-permute-start.14 = (bf16[2,1536,128]{2,1,0:T(8,128)(2,1)S(1)}, bf16[2,1536,128]{2,1,0:T(8,128)(2,1)S(1)}, u32[]{:S(2)}, u32[]{:S(2)}) collective-permute-start(bf16[2,1536,128]{2,1,0:T(8,128)(2,1)S(1)} %slice.48), channel_id=1, source_target_pairs={{0,12},{1,13},{2,14},{3,15},{4,0},{5,1},{6,2},{7,3},{8,4},{9,5},{1... | collective-permute-start | bytes 2359304 | tf_op jit(solution)/shard_map/ppermute | solution.py:46
  67.4 12.4 %collective-permute-start.13 = (bf16[2,1536,128]{2,1,0:T(8,128)(2,1)S(1)}, bf16[2,1536,128]{2,1,0:T(8,128)(2,1)S(1)}, u32[]{:S(2)}, u32[]{:S(2)}) collective-permute-start(bf16[2,1536,128]{2,1,0:T(8,128)(2,1)S(1)} %slice.47), channel_id=1, source_target_pairs={{0,4},{1,5},{2,6},{3,7},{4,8},{5,9},{6,10},{7,11},{8,12},{9,13},{1... | collective-permute-start | bytes 2359304 | tf_op jit(solution)/shard_map/ppermute | solution.py:46
  73.4 14.1 %collective-permute-start.6 = (bf16[2,1536,128]{2,1,0:T(8,128)(2,1)S(1)}, bf16[2,1536,128]{2,1,0:T(8,128)(2,1)S(1)}, u32[]{:S(2)}, u32[]{:S(2)}) collective-permute-start(bf16[2,1536,128]{2,1,0:T(8,128)(2,1)S(1)} %slice.45), channel_id=1, source_target_pairs={{0,12},{1,13},{2,14},{3,15},{4,0},{5,1},{6,2},{7,3},{8,4},{9,5},{1... | collective-permute-start | bytes 2359304 | tf_op jit(solution)/shard_map/ppermute | solution.py:46
  75.9 12.1 %collective-permute-start.5 = (bf16[2,1536,128]{2,1,0:T(8,128)(2,1)S(1)}, bf16[2,1536,128]{2,1,0:T(8,128)(2,1)S(1)}, u32[]{:S(2)}, u32[]{:S(2)}) collective-permute-start(bf16[2,1536,128]{2,1,0:T(8,128)(2,1)S(1)} %slice.44), channel_id=1, source_target_pairs={{0,4},{1,5},{2,6},{3,7},{4,8},{5,9},{6,10},{7,11},{8,12},{9,13},{1... | collective-permute-start | bytes 2359304 | tf_op jit(solution)/shard_map/ppermute | solution.py:46
  87.4 8.4 %copy-start.6 = (f32[1024,512]{1,0:T(8,128)S(1)}, f32[1024,512]{1,0:T(8,128)}, u32[]{:S(2)}) copy-start(f32[1024,512]{1,0:T(8,128)} %get-tuple-element.30.mine2) | copy-start | bytes 6291460
  87.4 8.3 %collective-permute-start.15 = (f32[1024,512]{1,0:T(8,128)}, f32[1024,512]{1,0:T(8,128)S(1)}, u32[]{:S(2)}, u32[]{:S(2)}) collective-permute-start(f32[1024,512]{1,0:T(8,128)} %get-tuple-element.31), channel_id=1, source_target_pairs={{0,16},{1,17},{2,18},{3,19},{4,20},{5,21},{6,22},{7,23},{8,24},{9,... | collective-permute-start | bytes 6291464 | tf_op jit(solution)/shard_map/ppermute | solution.py:46
  95.7 4.5 %collective-permute-start.7 = (f32[1024,512]{1,0:T(8,128)}, f32[1024,512]{1,0:T(8,128)S(1)}, u32[]{:S(2)}, u32[]{:S(2)}) collective-permute-start(f32[1024,512]{1,0:T(8,128)} %get-tuple-element.29), channel_id=1, source_target_pairs={{0,16},{1,17},{2,18},{3,19},{4,20},{5,21},{6,22},{7,23},{8,24},{9,... | collective-permute-start | bytes 6291464 | tf_op jit(solution)/shard_map/ppermute | solution.py:46
  100.1 18.0 %copy-start.9 = (f32[1024,512]{1,0:T(8,128)}, f32[1024,512]{1,0:T(8,128)S(1)}, u32[]{:S(2)}) copy-start(f32[1024,512]{1,0:T(8,128)S(1)} %collective-permute-done.7.came1) | copy-start | bytes 6291460
  100.4 17.8 %collective-permute-start.16 = (bf16[512,512]{1,0:T(8,128)(2,1)S(1)}, bf16[512,512]{1,0:T(8,128)(2,1)S(1)}, u32[]{:S(2)}, u32[]{:S(2)}) collective-permute-start(bf16[512,512]{1,0:T(8,128)(2,1)S(1)} %fusion.5), channel_id=1, source_target_pairs={{0,32},{1,33},{2,34},{3,35},{4,36},{5,37},{6,38},{7,39},{8,40},{9,... | collective-permute-start | bytes 1572872 | tf_op jit(solution)/shard_map/ppermute | solution.py:46
  106.2 12.2 %collective-permute-start.17 = (bf16[512,512]{1,0:T(8,128)(2,1)S(1)}, bf16[512,512]{1,0:T(8,128)(2,1)S(1)}, u32[]{:S(2)}, u32[]{:S(2)}) collective-permute-start(bf16[512,512]{1,0:T(8,128)(2,1)S(1)} %fusion.4), channel_id=1, source_target_pairs={{0,32},{1,33},{2,34},{3,35},{4,36},{5,37},{6,38},{7,39},{8,40},{9,... | collective-permute-start | bytes 1572872 | tf_op jit(solution)/shard_map/ppermute | solution.py:46
  118.2 4.8 %copy-start.11 = (bf16[512,512]{1,0:T(8,128)(2,1)}, bf16[512,512]{1,0:T(8,128)(2,1)S(1)}, u32[]{:S(2)}) copy-start(bf16[512,512]{1,0:T(8,128)(2,1)S(1)} %collective-permute-done.16.got1) | copy-start | bytes 1572868
  119.4 14.9 %all-to-all-start.1 = ((f32[16,1,6144]{2,1,0:T(1,128)}), f32[16,1,6144]{2,1,0:T(1,128)S(1)}, u32[]{:S(2)}, u32[]{:S(2)}) async-start(f32[16,1,6144]{2,1,0:T(1,128)} %broadcast_in_dim.10), calls=%async_computation.1 | async-start | bytes 786432 | tf_op jit(solution)/shard_map/all_to_all | solution.py:254
  126.6 28.4 %collective-permute-start.18 = (bf16[256,512]{1,0:T(8,128)(2,1)}, bf16[256,512]{1,0:T(8,128)(2,1)S(1)}, u32[]{:S(2)}, u32[]{:S(2)}) collective-permute-start(bf16[256,512]{1,0:T(8,128)(2,1)} %get-tuple-element.45), channel_id=1, source_target_pairs={{0,64},{1,65},{2,66},{3,67},{4,68},{5,69},{6,70},{7,71},{8,72},{9,... | collective-permute-start | bytes 786440 | tf_op jit(solution)/shard_map/ppermute | solution.py:46
  126.6 28.4 %collective-permute-start.19 = (bf16[256,512]{1,0:T(8,128)(2,1)}, bf16[256,512]{1,0:T(8,128)(2,1)S(1)}, u32[]{:S(2)}, u32[]{:S(2)}) collective-permute-start(bf16[256,512]{1,0:T(8,128)(2,1)} %get-tuple-element.46), channel_id=1, source_target_pairs={{0,192},{1,193},{2,194},{3,195},{4,196},{5,197},{6,198},{7,199},{8... | collective-permute-start | bytes 786440 | tf_op jit(solution)/shard_map/ppermute | solution.py:46
  130.2 24.8 %collective-permute-start.20 = (bf16[256,512]{1,0:T(8,128)(2,1)}, bf16[256,512]{1,0:T(8,128)(2,1)S(1)}, u32[]{:S(2)}, u32[]{:S(2)}) collective-permute-start(bf16[256,512]{1,0:T(8,128)(2,1)} %get-tuple-element.47), channel_id=1, source_target_pairs={{0,128},{1,129},{2,130},{3,131},{4,132},{5,133},{6,134},{7,135},{8... | collective-permute-start | bytes 786440 | tf_op jit(solution)/shard_map/ppermute | solution.py:46
  135.8 19.2 %all-to-all-start.2 = ((f32[16,1,512]{2,1,0:T(1,128)}), f32[16,1,512]{2,1,0:T(1,128)S(1)}, u32[]{:S(2)}, u32[]{:S(2)}) async-start(f32[16,1,512]{2,1,0:T(1,128)} %broadcast_in_dim.11), calls=%async_computation.2 | async-start | bytes 65536 | tf_op jit(solution)/shard_map/all_to_all | solution.py:254
  141.8 13.9 %copy-start.10 = (f32[256,512]{1,0:T(8,128)S(1)}, f32[256,512]{1,0:T(8,128)}, u32[]{:S(2)}) copy-start(f32[256,512]{1,0:T(8,128)} %get-tuple-element.42) | copy-start | bytes 1572868
  (5 other events, 22.4 us)

commit v2 on v0

--- a/solution.py
+++ b/solution.py
@@ -261,7 +261,7 @@
 def last_body(hidden, gate, grad, normalized, weight, inverse, products, grad_hidden, grad_gate):
     for t in range(hidden.shape[0] // 128):
         part = slice(t * 128, t * 128 + 128)
-        row = jnp.sum(products[:, part], axis=0, keepdims=True) / DI
+        row = jnp.sum(products[:, :, part], axis=0) / DI
         mean = jnp.broadcast_to(row, (128, 128)).T
         scale = jnp.broadcast_to(inverse[:, part], (128, 128)).T
         for k in range(hidden.shape[1] // 128):
@@ -286,7 +286,7 @@
             wide, wide, wide, wide,
             pl.BlockSpec((1, ch), lambda i: (0, 0)),
             pl.BlockSpec((1, tile), lambda i: (0, i)),
-            pl.BlockSpec((16, tile), lambda i: (0, i)),
+            pl.BlockSpec((16, 1, tile), lambda i: (0, 0, i)),
         ],
         out_specs=(wide, wide),
         cost_estimate=pl.CostEstimate(flops=1_000, bytes_accessed=1_000, transcendentals=0),
@@ -328,6 +328,7 @@
     inverse_rms = 1.0 / jnp.sqrt(squares / DI + 1e-05)
     normalized = gated * inverse_rms[:, None]
     normed = (normalized * norm_weight).astype(BF)
+    inverse_row, normed = lax.optimization_barrier((inverse_rms[None], normed))
 
     def grouped(operand, chunk, with_w, with_n):
         n = operand
@@ -352,9 +353,10 @@
     rows = own
     for block, d in zip((outs[1], outs[2], outs[0]), (2, -2, 4)):
         rows = rows + send(block, along_z(d)).astype(F32)
-    products = parts_of(stat, "tensor")
+    wide_stat = jnp.broadcast_to(stat[None], (16,) + stat.shape)
+    products = lax.all_to_all(wide_stat, "tensor", 0, 0, tiled=True)
     grad_hidden, grad_gate = last(
-        hidden_states, gate_values, grad_normed, normalized, norm_weight[None], inverse_rms[None], products
+        hidden_states, gate_values, grad_normed, normalized, norm_weight[None], inverse_row, products
     )
     gain, _ = lax.optimization_barrier((gain[0], products))
     grad_norm_weight = total(gain, "seq")

time: 158 us -> 158 us (level)
    all_to_all x0 -> x1, waiting for transfers between devices: none -> 6.75 us  [local(): products = lax.all_to_all(wide_stat, 'tensor', 0, 0, tiled=True)]
    all_to_all x3 -> x2, waiting for transfers between devices: 30.8 us -> 24.1 us  [parts_of(): return lax.all_to_all(spread, axis, 0, 0, tiled=True)]
    all_to_all x0 -> x1, starting transfers between devices: none -> 3.51 us  [local(): products = lax.all_to_all(wide_stat, 'tensor', 0, 0, tiled=True)]
    all_to_all x3 -> x2, starting transfers between devices: 14.8 us -> 11.3 us  [parts_of(): return lax.all_to_all(spread, axis, 0, 0, tiled=True)]
  transfers between devices with their start and end apart: 24 -> 24, of which waited for: 10 -> 11; matrix products, arithmetic and copies ran while one was open for 9% -> 9% of each run, Pallas kernels for 22% -> 22%
where the time goes in v2:
time: 158 us; the launch traced here: 157 us
  waiting for transfers between devices  54 us (34%)
  starting transfers between devices  45 us (28%)
  Pallas kernels  38 us (24%)
  local copies, waits for them, and re-layouts  9.98 us (6%)
  other arithmetic  6.93 us (4%)
  between operations  3.4 us (2%)
    ppermute x21, starting transfers between devices, send(): return lax.ppermute(value, AXES, table)  30.2 us
    pallas_call x3, Pallas kernels, block_kernel(): pl.pallas_call(lambda *refs: block_body(groups, len(stacks), has_acc, las...  27 us
    all_to_all x2, waiting for transfers between devices, parts_of(): return lax.all_to_all(spread, axis, 0, 0, tiled=True)  24.1 us
    ppermute x21, waiting for transfers between devices, send(): return lax.ppermute(value, AXES, table)  23.1 us
    all_to_all x2, starting transfers between devices, parts_of(): return lax.all_to_all(spread, axis, 0, 0, tiled=True)  11.3 us
    pallas_call x1, Pallas kernels, last(): pl.pallas_call(last_body, grid=(tok // tile,), out_shape=(jax.ShapeDtypeS...  7.41 us
    all_to_all x1, waiting for transfers between devices, local(): products = lax.all_to_all(wide_stat, 'tensor', 0, 0, tiled=True)  6.75 us
    pallas_call x1, Pallas kernels, mix(): pl.pallas_call(mix_body, grid=(1,), out_shape=(jax.ShapeDtypeStruct((2 *...  3.63 us
  transfers between devices with their start and end apart: 24, of which 11 were waited for; matrix products, arithmetic and copies ran while one was open for 9% of the time, Pallas kernels for 22%

profile of v2, /device:TPU:1, one launch (start us, length us, event | category | flops | bytes accessed | tf_op | source)
XLA Modules:
  0.0 157.3 jit_solution(15754838029206885038)
XLA Ops:
  0.6 1.3 slice_bitcast_fusion
  2.0 3.6 %collective-permute-start.9 = (bf16[1536,128]{1,0:T(8,128)(2,1)S(1)}, bf16[1536,128]{1,0:T(8,128)(2,1)S(1)}, u32[]{:S(2)}, u32[]{:S(2)}) collective-permute-start(bf16[1536,128]{1,0:T(8,128)(2,1)S(1)} %get-tuple-element.52), channel_id=1, source_target_pairs={{0,3},{1,0},{2,1},{3,2},{4,7},{5,4},{6,5},{7,6},{8,11},{9,8},{10,9... | collective-permute-start | bytes 1179656 | tf_op jit(solution)/shard_map/ppermute | solution.py:46
  5.6 1.6 %collective-permute-start.10 = (bf16[1536,128]{1,0:T(8,128)(2,1)S(1)}, bf16[1536,128]{1,0:T(8,128)(2,1)S(1)}, u32[]{:S(2)}, u32[]{:S(2)}) collective-permute-start(bf16[1536,128]{1,0:T(8,128)(2,1)S(1)} %get-tuple-element.52), channel_id=1, source_target_pairs={{0,2},{1,3},{2,0},{3,1},{4,6},{5,7},{6,4},{7,5},{8,10},{9,11},{10,... | collective-permute-start | bytes 1179656 | tf_op jit(solution)/shard_map/ppermute | solution.py:46
  8.9 5.7 %collective-permute-done.9 = bf16[1536,128]{1,0:T(8,128)(2,1)S(1)} collective-permute-done((bf16[1536,128]{1,0:T(8,128)(2,1)S(1)}, bf16[1536,128]{1,0:T(8,128)(2,1)S(1)}, u32[]{:S(2)}, u32[]{:S(2)}) %collective-permute-start.9) | collective-permute-done | bytes 393248 | tf_op jit(solution)/shard_map/ppermute | solution.py:46
  14.5 3.4 %collective-permute-done.8 = bf16[1536,128]{1,0:T(8,128)(2,1)S(1)} collective-permute-done((bf16[1536,128]{1,0:T(8,128)(2,1)S(1)}, bf16[1536,128]{1,0:T(8,128)(2,1)S(1)}, u32[]{:S(2)}, u32[]{:S(2)}) %collective-permute-start.8) | collective-permute-done | bytes 393248 | tf_op jit(solution)/shard_map/ppermute | solution.py:46
  18.2 2.6 %collective-permute-start.12 = (bf16[4,1536,128]{2,1,0:T(8,128)(2,1)S(1)}, bf16[4,1536,128]{2,1,0:T(8,128)(2,1)}, u32[]{:S(2)}, u32[]{:S(2)}) collective-permute-start(bf16[4,1536,128]{2,1,0:T(8,128)(2,1)S(1)} %pad_maximum_fusion.1.refs_1_.refs_6_), channel_id=1, source_target_pairs={{0,12},{1,13},{2,14},{3,15},{4,0},{5,1},{6,2},{7,3},{8,4},{9,5},{1... | collective-permute-start | bytes 4718600 | tf_op jit(solution)/shard_map/ppermute | solution.py:46
  20.7 5.6 %collective-permute-done = bf16[1536,128]{1,0:T(8,128)(2,1)S(1)} collective-permute-done((bf16[1536,128]{1,0:T(8,128)(2,1)S(1)}, bf16[1536,128]{1,0:T(8,128)(2,1)S(1)}, u32[]{:S(2)}, u32[]{:S(2)}) %collective-permute-start) | collective-permute-done | bytes 393248 | tf_op jit(solution)/shard_map/ppermute | solution.py:46
  26.6 3.5 %collective-permute-start.4 = (bf16[4,1536,128]{2,1,0:T(8,128)(2,1)S(1)}, bf16[4,1536,128]{2,1,0:T(8,128)(2,1)}, u32[]{:S(2)}, u32[]{:S(2)}) collective-permute-start(bf16[4,1536,128]{2,1,0:T(8,128)(2,1)S(1)} %pad_maximum_fusion.refs_1_), channel_id=1, source_target_pairs={{0,12},{1,13},{2,14},{3,15},{4,0},{5,1},{6,2},{7,3},{8,4},{9,5},{1... | collective-permute-start | bytes 4718600 | tf_op jit(solution)/shard_map/ppermute | solution.py:46
  30.1 1.1 multiply_reduce_fusion
  31.9 6.0 %all-to-all-start = ((f32[16,1,1536]{2,1,0:T(1,128)}), f32[16,1,1536]{2,1,0:T(1,128)S(1)}, u32[]{:S(2)}, u32[]{:S(2)}) async-start(f32[16,1,1536]{2,1,0:T(1,128)} %broadcast_in_dim.10), calls=%async_computation | async-start | bytes 196608 | tf_op jit(solution)/shard_map/all_to_all | solution.py:254
  40.5 24.0 %all-to-all-done = f32[16,1,1536]{2,1,0:T(1,128)S(1)} async-done(((f32[16,1,1536]{2,1,0:T(1,128)}), f32[16,1,1536]{2,1,0:T(1,128)S(1)}, u32[]{:S(2)}, u32[]{:S(2)}) %all-to-all-start) | async-done | bytes 98336 | tf_op jit(solution)/shard_map/all_to_all | solution.py:254
  65.2 1.5 slice.48
  67.0 1.2 slice.47
  68.2 1.5 collective-permute-start.13
  69.7 3.3 %multiply_convert_fusion = (bf16[1536,512]{1,0:T(8,128)(2,1)}, f32[1536,512]{1,0:T(8,128)}) fusion(f32[512]{0:T(512)S(1)} %copy-done.1, f32[1536]{0:T(1024)S(1)} %add_rsqrt_fusion, bf16[1536,512]{1,0:T(8,128)(2,1)S(1)} %copy-done.5, bf16[1536,512]{1,0:T(8,128)(2,1)S(1)} %copy-done.3), kind=kLoop, calls=%fused_computation.6 | loop fusion | flops 7864320 | bytes 7872512 | tf_op jit(solution)/shard_map/convert_element_type | solution.py:330
  73.0 1.2 slice.45
  74.2 1.3 collective-permute-start.6
  75.5 1.2 slice.44
  77.0 1.1 collective-permute-done.14.refs_5_.refs_10_
  78.1 2.5 %collective-permute-done.13.refs_4_.refs_9_ = bf16[2,1536,128]{2,1,0:T(8,128)(2,1)S(1)} collective-permute-done((bf16[2,1536,128]{2,1,0:T(8,128)(2,1)S(1)}, bf16[2,1536,128]{2,1,0:T(8,128)(2,1)S(1)}, u32[]{:S(2)}, u32[]{:S(2)}) %collective-permute-start.13) | collective-permute-done | bytes 786464 | tf_op jit(solution)/shard_map/ppermute | solution.py:46
  80.6 7.6 %outer2.1 = (f32[1024,512]{1,0:T(8,128)}, f32[1024,512]{1,0:T(8,128)}) custom-call(s32[32]{0:T(128)S(1)} %stack.161.refs_0_, bf16[4,1536,128]{2,1,0:T(8,128)(2,1)S(1)} %pad_maximum_fusion.1.refs_1_.refs_6_, bf16[4,1536,128]{2,1,0:T(8,128)(2,1)} %collective-permute-done.11.refs_2_.refs_7_, bf16[4,1536,128]{2,1,0:T(8,128)(2,1)} %collective-permute-done.12.refs_3_.refs_8_, ...), custom_call_target="tpu_custom_call" | custom-call | flops 32000000000 | bytes 96000000 | tf_op jit(solution)/shard_map/outer2/pallas_call | solution.py:217
  88.8 7.6 %outer1.1 = (f32[1024,512]{1,0:T(8,128)}, f32[1024,512]{1,0:T(8,128)}) custom-call(s32[32]{0:T(128)S(1)} %stack.161.refs_0_, bf16[4,1536,128]{2,1,0:T(8,128)(2,1)S(1)} %pad_maximum_fusion.refs_1_, bf16[4,1536,128]{2,1,0:T(8,128)(2,1)} %collective-permute-done.3.refs_2_, bf16[4,1536,128]{2,1,0:T(8,128)(2,1)} %collective-permute-done.4.refs_3_, ...), custom_call_target="tpu_custom_call" | custom-call | flops 32000000000 | bytes 96000000 | tf_op jit(solution)/shard_map/outer1/pallas_call | solution.py:217
  96.8 4.1 %collective-permute-done.7.came1 = f32[1024,512]{1,0:T(8,128)S(1)} collective-permute-done((f32[1024,512]{1,0:T(8,128)}, f32[1024,512]{1,0:T(8,128)S(1)}, u32[]{:S(2)}, u32[]{:S(2)}) %collective-permute-start.7) | collective-permute-done | bytes 2097184 | tf_op jit(solution)/shard_map/ppermute | solution.py:46
  101.1 5.8 %collective-permute-start.16 = (bf16[512,512]{1,0:T(8,128)(2,1)S(1)}, bf16[512,512]{1,0:T(8,128)(2,1)S(1)}, u32[]{:S(2)}, u32[]{:S(2)}) collective-permute-start(bf16[512,512]{1,0:T(8,128)(2,1)S(1)} %fusion.5), channel_id=1, source_target_pairs={{0,32},{1,33},{2,34},{3,35},{4,36},{5,37},{6,38},{7,39},{8,40},{9,... | collective-permute-start | bytes 1572872 | tf_op jit(solution)/shard_map/ppermute | solution.py:46
  107.1 11.9 %inner.1 = (f32[1536,512]{1,0:T(8,128)}, f32[1,1536]{1,0:T(1,128)S(1)}, f32[8,512]{1,0:T(8,128)S(1)}) custom-call(s32[32]{0:T(128)S(1)} %stack.161.refs_0_, bf16[4,1536,128]{2,1,0:T(8,128)(2,1)S(1)} %pad_maximum_fusion.refs_1_, bf16[4,1536,128]{2,1,0:T(8,128)(2,1)} %collective-permute-done.3.refs_2_, bf16[4,1536,128]{2,1,0:T(8,128)(2,1)} %collective-permute-done.4.refs_3_, ...), custom_call_target="tpu_custom_call" | custom-call | flops 64000000000 | bytes 192000000 | tf_op jit(solution)/shard_map/inner/pallas_call | solution.py:217
  119.9 3.6 %mix.1 = (f32[256,512]{1,0:T(8,128)}, bf16[256,512]{1,0:T(8,128)(2,1)}, bf16[256,512]{1,0:T(8,128)(2,1)}, bf16[256,512]{1,0:T(8,128)(2,1)}) custom-call(f32[1024,512]{1,0:T(8,128)} %get-tuple-element.27.mine1, f32[1024,512]{1,0:T(8,128)} %copy-done.9, bf16[512,512]{1,0:T(8,128)(2,1)} %copy-done.11, f32[1024,512]{1,0:T(8,128)} %get-tuple-element.29.mine2, ...), custom_call_target="tpu_custom_call" | custom-call | flops 4000000 | bytes 8000000 | tf_op jit(solution)/shard_map/mix/pallas_call | solution.py:241
  123.6 3.6 %collective-permute-start.19 = (bf16[256,512]{1,0:T(8,128)(2,1)}, bf16[256,512]{1,0:T(8,128)(2,1)S(1)}, u32[]{:S(2)}, u32[]{:S(2)}) collective-permute-start(bf16[256,512]{1,0:T(8,128)(2,1)} %get-tuple-element.44), channel_id=1, source_target_pairs={{0,192},{1,193},{2,194},{3,195},{4,196},{5,197},{6,198},{7,199},{8... | collective-permute-start | bytes 786440 | tf_op jit(solution)/shard_map/ppermute | solution.py:46
  127.2 4.1 %collective-permute-start.20 = (bf16[256,512]{1,0:T(8,128)(2,1)}, bf16[256,512]{1,0:T(8,128)(2,1)S(1)}, u32[]{:S(2)}, u32[]{:S(2)}) collective-permute-start(bf16[256,512]{1,0:T(8,128)(2,1)} %get-tuple-element.45), channel_id=1, source_target_pairs={{0,128},{1,129},{2,130},{3,131},{4,132},{5,133},{6,134},{7,135},{8... | collective-permute-start | bytes 786440 | tf_op jit(solution)/shard_map/ppermute | solution.py:46
  131.9 3.5 %all-to-all-start.1 = ((f32[16,1,1536]{2,1,0:T(1,128)}), f32[16,1,1536]{2,1,0:T(1,128)S(1)}, u32[]{:S(2)}, u32[]{:S(2)}) async-start(f32[16,1,1536]{2,1,0:T(1,128)} %broadcast_in_dim.13), calls=%async_computation.1 | async-start | bytes 196608 | tf_op jit(solution)/shard_map/all_to_all | solution.py:357
  135.5 6.8 %all-to-all-done.1.products = f32[16,1,1536]{2,1,0:T(1,128)S(1)} async-done(((f32[16,1,1536]{2,1,0:T(1,128)}), f32[16,1,1536]{2,1,0:T(1,128)S(1)}, u32[]{:S(2)}, u32[]{:S(2)}) %all-to-all-start.1) | async-done | bytes 98336 | tf_op jit(solution)/shard_map/all_to_all | solution.py:357
  142.9 5.3 %all-to-all-start.2 = ((f32[16,1,512]{2,1,0:T(1,128)}), f32[16,1,512]{2,1,0:T(1,128)S(1)}, u32[]{:S(2)}, u32[]{:S(2)}) async-start(f32[16,1,512]{2,1,0:T(1,128)} %broadcast_in_dim.14), calls=%async_computation.2 | async-start | bytes 65536 | tf_op jit(solution)/shard_map/all_to_all | solution.py:254
  148.2 7.4 %last.1 = (bf16[1536,512]{1,0:T(8,128)(2,1)}, bf16[1536,512]{1,0:T(8,128)(2,1)}) custom-call(bf16[1536,512]{1,0:T(8,128)(2,1)} %hidden.1, bf16[1536,512]{1,0:T(8,128)(2,1)} %gate.1, f32[1536,512]{1,0:T(8,128)} %get-tuple-element.32.grad, f32[1536,512]{1,0:T(8,128)} %get-tuple-element.49.refs_13_.normalized, f32[1,512]{1,0:T(1,128)} %bitcast.44, ...), custom_call_target="tpu_custom_call" | custom-call | flops 1000 | bytes 1000 | tf_op jit(solution)/shard_map/last/pallas_call | solution.py:281
  (71 shorter events, 9.5 us)
Async XLA Ops:
  2.0 12.6 %collective-permute-start.9 = (bf16[1536,128]{1,0:T(8,128)(2,1)S(1)}, bf16[1536,128]{1,0:T(8,128)(2,1)S(1)}, u32[]{:S(2)}, u32[]{:S(2)}) collective-permute-start(bf16[1536,128]{1,0:T(8,128)(2,1)S(1)} %get-tuple-element.52), channel_id=1, source_target_pairs={{0,3},{1,0},{2,1},{3,2},{4,7},{5,4},{6,5},{7,6},{8,11},{9,8},{10,9... | collective-permute-start | bytes 1179656 | tf_op jit(solution)/shard_map/ppermute | solution.py:46
  5.6 12.3 %collective-permute-start.8 = (bf16[1536,128]{1,0:T(8,128)(2,1)S(1)}, bf16[1536,128]{1,0:T(8,128)(2,1)S(1)}, u32[]{:S(2)}, u32[]{:S(2)}) collective-permute-start(bf16[1536,128]{1,0:T(8,128)(2,1)S(1)} %get-tuple-element.52), channel_id=1, source_target_pairs={{0,1},{1,2},{2,3},{3,0},{4,5},{5,6},{6,7},{7,4},{8,9},{9,10},{10,1... | collective-permute-start | bytes 1179656 | tf_op jit(solution)/shard_map/ppermute | solution.py:46
  5.6 12.3 %collective-permute-start.10 = (bf16[1536,128]{1,0:T(8,128)(2,1)S(1)}, bf16[1536,128]{1,0:T(8,128)(2,1)S(1)}, u32[]{:S(2)}, u32[]{:S(2)}) collective-permute-start(bf16[1536,128]{1,0:T(8,128)(2,1)S(1)} %get-tuple-element.52), channel_id=1, source_target_pairs={{0,2},{1,3},{2,0},{3,1},{4,6},{5,7},{6,4},{7,5},{8,10},{9,11},{10,... | collective-permute-start | bytes 1179656 | tf_op jit(solution)/shard_map/ppermute | solution.py:46
  7.2 13.5 %collective-permute-start.1 = (bf16[1536,128]{1,0:T(8,128)(2,1)S(1)}, bf16[1536,128]{1,0:T(8,128)(2,1)S(1)}, u32[]{:S(2)}, u32[]{:S(2)}) collective-permute-start(bf16[1536,128]{1,0:T(8,128)(2,1)S(1)} %get-tuple-element.53), channel_id=1, source_target_pairs={{0,3},{1,0},{2,1},{3,2},{4,7},{5,4},{6,5},{7,6},{8,11},{9,8},{10,9... | collective-permute-start | bytes 1179656 | tf_op jit(solution)/shard_map/ppermute | solution.py:46
  8.3 18.1 %collective-permute-start = (bf16[1536,128]{1,0:T(8,128)(2,1)S(1)}, bf16[1536,128]{1,0:T(8,128)(2,1)S(1)}, u32[]{:S(2)}, u32[]{:S(2)}) collective-permute-start(bf16[1536,128]{1,0:T(8,128)(2,1)S(1)} %get-tuple-element.53), channel_id=1, source_target_pairs={{0,1},{1,2},{2,3},{3,0},{4,5},{5,6},{6,7},{7,4},{8,9},{9,10},{10,1... | collective-permute-start | bytes 1179656 | tf_op jit(solution)/shard_map/ppermute | solution.py:46
  14.5 11.8 %collective-permute-start.2 = (bf16[1536,128]{1,0:T(8,128)(2,1)S(1)}, bf16[1536,128]{1,0:T(8,128)(2,1)S(1)}, u32[]{:S(2)}, u32[]{:S(2)}) collective-permute-start(bf16[1536,128]{1,0:T(8,128)(2,1)S(1)} %get-tuple-element.53), channel_id=1, source_target_pairs={{0,2},{1,3},{2,0},{3,1},{4,6},{5,7},{6,4},{7,5},{8,10},{9,11},{10,... | collective-permute-start | bytes 1179656 | tf_op jit(solution)/shard_map/ppermute | solution.py:46
  18.1 62.5 %copy-start = (bf16[4,1536,128]{2,1,0:T(8,128)(2,1)}, bf16[4,1536,128]{2,1,0:T(8,128)(2,1)S(1)}, u32[]{:S(2)}) copy-start(bf16[4,1536,128]{2,1,0:T(8,128)(2,1)S(1)} %pad_maximum_fusion.1.refs_1_.refs_6_) | copy-start | bytes 4718596
  18.2 12.0 %copy-start.2 = (bf16[1536,512]{1,0:T(8,128)(2,1)S(1)}, bf16[1536,512]{1,0:T(8,128)(2,1)}, u32[]{:S(2)}) copy-start(bf16[1536,512]{1,0:T(8,128)(2,1)} %hidden.1) | copy-start | bytes 4718596
  18.2 11.9 %copy-start.4 = (bf16[1536,512]{1,0:T(8,128)(2,1)S(1)}, bf16[1536,512]{1,0:T(8,128)(2,1)}, u32[]{:S(2)}) copy-start(bf16[1536,512]{1,0:T(8,128)(2,1)} %gate.1) | copy-start | bytes 4718596
  18.2 47.0 %collective-permute-start.12 = (bf16[4,1536,128]{2,1,0:T(8,128)(2,1)S(1)}, bf16[4,1536,128]{2,1,0:T(8,128)(2,1)}, u32[]{:S(2)}, u32[]{:S(2)}) collective-permute-start(bf16[4,1536,128]{2,1,0:T(8,128)(2,1)S(1)} %pad_maximum_fusion.1.refs_1_.refs_6_), channel_id=1, source_target_pairs={{0,12},{1,13},{2,14},{3,15},{4,0},{5,1},{6,2},{7,3},{8,4},{9,5},{1... | collective-permute-start | bytes 4718600 | tf_op jit(solution)/shard_map/ppermute | solution.py:46
  20.7 46.2 %collective-permute-start.11 = (bf16[4,1536,128]{2,1,0:T(8,128)(2,1)S(1)}, bf16[4,1536,128]{2,1,0:T(8,128)(2,1)}, u32[]{:S(2)}, u32[]{:S(2)}) collective-permute-start(bf16[4,1536,128]{2,1,0:T(8,128)(2,1)S(1)} %pad_maximum_fusion.1.refs_1_.refs_6_), channel_id=1, source_target_pairs={{0,4},{1,5},{2,6},{3,7},{4,8},{5,9},{6,10},{7,11},{8,12},{9,13},{1... | collective-permute-start | bytes 4718600 | tf_op jit(solution)/shard_map/ppermute | solution.py:46
  26.6 46.4 %collective-permute-start.4 = (bf16[4,1536,128]{2,1,0:T(8,128)(2,1)S(1)}, bf16[4,1536,128]{2,1,0:T(8,128)(2,1)}, u32[]{:S(2)}, u32[]{:S(2)}) collective-permute-start(bf16[4,1536,128]{2,1,0:T(8,128)(2,1)S(1)} %pad_maximum_fusion.refs_1_), channel_id=1, source_target_pairs={{0,12},{1,13},{2,14},{3,15},{4,0},{5,1},{6,2},{7,3},{8,4},{9,5},{1... | collective-permute-start | bytes 4718600 | tf_op jit(solution)/shard_map/ppermute | solution.py:46
  30.1 45.4 %collective-permute-start.3 = (bf16[4,1536,128]{2,1,0:T(8,128)(2,1)S(1)}, bf16[4,1536,128]{2,1,0:T(8,128)(2,1)}, u32[]{:S(2)}, u32[]{:S(2)}) collective-permute-start(bf16[4,1536,128]{2,1,0:T(8,128)(2,1)S(1)} %pad_maximum_fusion.refs_1_), channel_id=1, source_target_pairs={{0,4},{1,5},{2,6},{3,7},{4,8},{5,9},{6,10},{7,11},{8,12},{9,13},{1... | collective-permute-start | bytes 4718600 | tf_op jit(solution)/shard_map/ppermute | solution.py:46
  31.9 32.6 %all-to-all-start = ((f32[16,1,1536]{2,1,0:T(1,128)}), f32[16,1,1536]{2,1,0:T(1,128)S(1)}, u32[]{:S(2)}, u32[]{:S(2)}) async-start(f32[16,1,1536]{2,1,0:T(1,128)} %broadcast_in_dim.10), calls=%async_computation | async-start | bytes 196608 | tf_op jit(solution)/shard_map/all_to_all | solution.py:254
  39.5 30.2 %copy-start.1 = (f32[512]{0:T(512)S(1)}, f32[512]{0:T(512)}, u32[]{:S(2)}) copy-start(f32[512]{0:T(512)} %param.7) | copy-start | bytes 6148
  66.7 11.4 %collective-permute-start.14 = (bf16[2,1536,128]{2,1,0:T(8,128)(2,1)S(1)}, bf16[2,1536,128]{2,1,0:T(8,128)(2,1)S(1)}, u32[]{:S(2)}, u32[]{:S(2)}) collective-permute-start(bf16[2,1536,128]{2,1,0:T(8,128)(2,1)S(1)} %slice.48), channel_id=1, source_target_pairs={{0,12},{1,13},{2,14},{3,15},{4,0},{5,1},{6,2},{7,3},{8,4},{9,5},{1... | collective-permute-start | bytes 2359304 | tf_op jit(solution)/shard_map/ppermute | solution.py:46
  68.2 12.4 %collective-permute-start.13 = (bf16[2,1536,128]{2,1,0:T(8,128)(2,1)S(1)}, bf16[2,1536,128]{2,1,0:T(8,128)(2,1)S(1)}, u32[]{:S(2)}, u32[]{:S(2)}) collective-permute-start(bf16[2,1536,128]{2,1,0:T(8,128)(2,1)S(1)} %slice.47), channel_id=1, source_target_pairs={{0,4},{1,5},{2,6},{3,7},{4,8},{5,9},{6,10},{7,11},{8,12},{9,13},{1... | collective-permute-start | bytes 2359304 | tf_op jit(solution)/shard_map/ppermute | solution.py:46
  74.2 14.1 %collective-permute-start.6 = (bf16[2,1536,128]{2,1,0:T(8,128)(2,1)S(1)}, bf16[2,1536,128]{2,1,0:T(8,128)(2,1)S(1)}, u32[]{:S(2)}, u32[]{:S(2)}) collective-permute-start(bf16[2,1536,128]{2,1,0:T(8,128)(2,1)S(1)} %slice.45), channel_id=1, source_target_pairs={{0,12},{1,13},{2,14},{3,15},{4,0},{5,1},{6,2},{7,3},{8,4},{9,5},{1... | collective-permute-start | bytes 2359304 | tf_op jit(solution)/shard_map/ppermute | solution.py:46
  76.7 12.1 %collective-permute-start.5 = (bf16[2,1536,128]{2,1,0:T(8,128)(2,1)S(1)}, bf16[2,1536,128]{2,1,0:T(8,128)(2,1)S(1)}, u32[]{:S(2)}, u32[]{:S(2)}) collective-permute-start(bf16[2,1536,128]{2,1,0:T(8,128)(2,1)S(1)} %slice.44), channel_id=1, source_target_pairs={{0,4},{1,5},{2,6},{3,7},{4,8},{5,9},{6,10},{7,11},{8,12},{9,13},{1... | collective-permute-start | bytes 2359304 | tf_op jit(solution)/shard_map/ppermute | solution.py:46
  88.2 8.4 %copy-start.6 = (f32[1024,512]{1,0:T(8,128)S(1)}, f32[1024,512]{1,0:T(8,128)}, u32[]{:S(2)}) copy-start(f32[1024,512]{1,0:T(8,128)} %get-tuple-element.29.mine2) | copy-start | bytes 6291460
  88.2 8.3 %collective-permute-start.15 = (f32[1024,512]{1,0:T(8,128)}, f32[1024,512]{1,0:T(8,128)S(1)}, u32[]{:S(2)}, u32[]{:S(2)}) collective-permute-start(f32[1024,512]{1,0:T(8,128)} %get-tuple-element.30), channel_id=1, source_target_pairs={{0,16},{1,17},{2,18},{3,19},{4,20},{5,21},{6,22},{7,23},{8,24},{9,... | collective-permute-start | bytes 6291464 | tf_op jit(solution)/shard_map/ppermute | solution.py:46
  96.4 4.5 %collective-permute-start.7 = (f32[1024,512]{1,0:T(8,128)}, f32[1024,512]{1,0:T(8,128)S(1)}, u32[]{:S(2)}, u32[]{:S(2)}) collective-permute-start(f32[1024,512]{1,0:T(8,128)} %get-tuple-element.28), channel_id=1, source_target_pairs={{0,16},{1,17},{2,18},{3,19},{4,20},{5,21},{6,22},{7,23},{8,24},{9,... | collective-permute-start | bytes 6291464 | tf_op jit(solution)/shard_map/ppermute | solution.py:46
  100.9 18.1 %copy-start.9 = (f32[1024,512]{1,0:T(8,128)}, f32[1024,512]{1,0:T(8,128)S(1)}, u32[]{:S(2)}) copy-start(f32[1024,512]{1,0:T(8,128)S(1)} %collective-permute-done.7.came1) | copy-start | bytes 6291460
  101.1 17.8 %collective-permute-start.16 = (bf16[512,512]{1,0:T(8,128)(2,1)S(1)}, bf16[512,512]{1,0:T(8,128)(2,1)S(1)}, u32[]{:S(2)}, u32[]{:S(2)}) collective-permute-start(bf16[512,512]{1,0:T(8,128)(2,1)S(1)} %fusion.5), channel_id=1, source_target_pairs={{0,32},{1,33},{2,34},{3,35},{4,36},{5,37},{6,38},{7,39},{8,40},{9,... | collective-permute-start | bytes 1572872 | tf_op jit(solution)/shard_map/ppermute | solution.py:46
  107.0 12.2 %collective-permute-start.17 = (bf16[512,512]{1,0:T(8,128)(2,1)S(1)}, bf16[512,512]{1,0:T(8,128)(2,1)S(1)}, u32[]{:S(2)}, u32[]{:S(2)}) collective-permute-start(bf16[512,512]{1,0:T(8,128)(2,1)S(1)} %fusion.4), channel_id=1, source_target_pairs={{0,32},{1,33},{2,34},{3,35},{4,36},{5,37},{6,38},{7,39},{8,40},{9,... | collective-permute-start | bytes 1572872 | tf_op jit(solution)/shard_map/ppermute | solution.py:46
  123.6 32.8 %collective-permute-start.18 = (bf16[256,512]{1,0:T(8,128)(2,1)}, bf16[256,512]{1,0:T(8,128)(2,1)S(1)}, u32[]{:S(2)}, u32[]{:S(2)}) collective-permute-start(bf16[256,512]{1,0:T(8,128)(2,1)} %get-tuple-element.43), channel_id=1, source_target_pairs={{0,64},{1,65},{2,66},{3,67},{4,68},{5,69},{6,70},{7,71},{8,72},{9,... | collective-permute-start | bytes 786440 | tf_op jit(solution)/shard_map/ppermute | solution.py:46
  123.6 32.8 %collective-permute-start.19 = (bf16[256,512]{1,0:T(8,128)(2,1)}, bf16[256,512]{1,0:T(8,128)(2,1)S(1)}, u32[]{:S(2)}, u32[]{:S(2)}) collective-permute-start(bf16[256,512]{1,0:T(8,128)(2,1)} %get-tuple-element.44), channel_id=1, source_target_pairs={{0,192},{1,193},{2,194},{3,195},{4,196},{5,197},{6,198},{7,199},{8... | collective-permute-start | bytes 786440 | tf_op jit(solution)/shard_map/ppermute | solution.py:46
  127.2 29.2 %collective-permute-start.20 = (bf16[256,512]{1,0:T(8,128)(2,1)}, bf16[256,512]{1,0:T(8,128)(2,1)S(1)}, u32[]{:S(2)}, u32[]{:S(2)}) collective-permute-start(bf16[256,512]{1,0:T(8,128)(2,1)} %get-tuple-element.45), channel_id=1, source_target_pairs={{0,128},{1,129},{2,130},{3,131},{4,132},{5,133},{6,134},{7,135},{8... | collective-permute-start | bytes 786440 | tf_op jit(solution)/shard_map/ppermute | solution.py:46
  131.9 10.3 %all-to-all-start.1 = ((f32[16,1,1536]{2,1,0:T(1,128)}), f32[16,1,1536]{2,1,0:T(1,128)S(1)}, u32[]{:S(2)}, u32[]{:S(2)}) async-start(f32[16,1,1536]{2,1,0:T(1,128)} %broadcast_in_dim.13), calls=%async_computation.1 | async-start | bytes 196608 | tf_op jit(solution)/shard_map/all_to_all | solution.py:357
  142.2 6.0 %copy-start.13 = (f32[16,1,1536]{2,1,0:T(1,128)}, f32[16,1,1536]{2,1,0:T(1,128)S(1)}, u32[]{:S(2)}) copy-start(f32[16,1,1536]{2,1,0:T(1,128)S(1)} %all-to-all-done.1.products) | copy-start | bytes 294916
  142.9 12.9 %all-to-all-start.2 = ((f32[16,1,512]{2,1,0:T(1,128)}), f32[16,1,512]{2,1,0:T(1,128)S(1)}, u32[]{:S(2)}, u32[]{:S(2)}) async-start(f32[16,1,512]{2,1,0:T(1,128)} %broadcast_in_dim.14), calls=%async_computation.2 | async-start | bytes 65536 | tf_op jit(solution)/shard_map/all_to_all | solution.py:254
  148.2 8.2 %copy-start.10 = (f32[256,512]{1,0:T(8,128)S(1)}, f32[256,512]{1,0:T(8,128)}, u32[]{:S(2)}) copy-start(f32[256,512]{1,0:T(8,128)} %get-tuple-element.42) | copy-start | bytes 1572868
  (6 other events, 21.1 us)
